TPU v7x, 512 devices: a whole 4x8x8 slice. The times are simulated.
512 devices in a mesh: seq: 8 (over z), chan: 16 (over y_hi, x, core), frame: 4 (over y_lo).
Axes of the slice: x: 4, y: 8 (y_hi: 2, y_lo: 4; y = y_hi * 4 + y_lo), z: 8, core: 2. Of those that a mesh axis runs over, the one named last changes fastest.
Arguments:
- token_qkv: bfloat16 [16, 8, 64, 3, 24, 128], P('chan', 'frame', 'seq'), may hold values from -8 to 8
- text_kv: bfloat16 [16, 256, 2, 24, 128], P('chan', 'seq'), may hold values from -6 to 6
- residual: bfloat16 [16, 8, 64, 3072], P('chan', 'frame', 'seq'), may hold values from -6 to 6
- query_gain: float32 [128], replicated, may hold values from 1.5 to 6
- key_gain: float32 [128], replicated, may hold values from 1.5 to 6
- out_weight: bfloat16 [24, 128, 3072], P('seq'), may hold values from -0.109375 to 0.109375
- res_gate: float32 [16, 3072], P('chan'), may hold values from 0.5 to 2
- mod_shift: float32 [16, 3072], P('chan'), may hold values from -3 to 3
- mod_scale: float32 [16, 3072], P('chan'), may hold values from -0.9 to 0.9
- final_weight: bfloat16 [64, 3072], replicated, may hold values from -0.109375 to 0.109375
- final_bias: float32 [64], replicated, may hold values from -1.5 to 1.5
- text_len: int32 [16], P('chan'), may hold values from 1 to 256, as said below
- video_frames: int32 [16], P('chan'), may hold values from 1 to 8, as said below
- in_weight: bfloat16 [27, 16, 512], P(None, None, 'chan'), may hold values from -0.3125 to 0.3125
- in_bias: float32 [512], P('chan'), may hold values from -1.5 to 1.5
- group_gain: float32 [512], P('chan'), may hold values from 0.1 to 1.9
- group_bias: float32 [512], P('chan'), may hold values from -1.5 to 1.5
- conv_weight: bfloat16 [27, 512, 512], P(None, None, 'chan'), may hold values from -0.0546875 to 0.0546875
- conv_bias: float32 [512], P('chan'), may hold values from -1.5 to 1.5
Outputs:
- decoded: bfloat16 [16, 8, 512, 256], P('seq', 'frame', 'chan')
Inputs may be any that keep to these rules, and one draw needn't show every extreme that they name: Text tokens at or past text_len of their video are padding; some video uses all 256 slots and some only one. latent frames at or past video_frames of their video are padding for the keys; some video uses all 8 frames and some only one.
All inputs are finite; a program needn't handle non-finite values.
Results may differ from a plain program's by a relative error of at most 0.022.
Values may be sent and summed in bfloat16 or wider, within the bound.
No kernel may reach another device: no remote copies, remote signals or barrier semaphores. Data moves between devices by JAX's collectives and lax.ppermute only.
A program may use at most 128 MiB of HBM per device.

v0:
```python
import math

import jax
import jax.numpy as jnp
from jax import lax
from jax.sharding import PartitionSpec as P

HD = 128
TXT = 256
LCH = 16
DCH = 512
GROUPS = 32
PH = 4
PW = 16


EPSILON = 1e-06


def passed_along(block, axis, distance):
    devices = range(lax.axis_size(axis))
    route = [(i - distance, i) for i in devices if i - distance in devices]
    return lax.ppermute(block, axis, route)


def rms_scale(values, row_gain):
    values = values.astype(jnp.float32)
    mean_square = jnp.mean(values * values, axis=-1, keepdims=True)
    return values * lax.rsqrt(mean_square + EPSILON) * row_gain


def conv_taps(volume, weight, frames_out):
    channels = volume.shape[0]
    height = volume.shape[3]
    breadth = volume.shape[4]
    padded = jnp.pad(volume, ((0, 0), (0, 0), (0, 0), (1, 1), (1, 1)))
    windows = []
    for tap_index in range(27):
        step_t = tap_index // 9
        step_y = tap_index // 3 % 3
        step_x = tap_index % 3
        window = padded[
            :, :, step_t : step_t + frames_out, step_y : step_y + height, step_x : step_x + breadth
        ]
        windows.append(window.reshape(channels, -1))
    stacked = jnp.concatenate(windows, axis=0)
    flat_weight = weight.reshape(27 * channels, weight.shape[2])
    return lax.dot_general(
        flat_weight, stacked, (((0,), (0,)), ((), ())), preferred_element_type=jnp.float32
    )


def causal_edge(volume, arrived):
    lead_frame = volume[:, :, :1]
    repeated = jnp.concatenate([lead_frame, lead_frame], axis=2)
    earlier = jnp.where(lax.axis_index("frame") == 0, repeated, arrived)
    return jnp.concatenate([earlier, volume], axis=2)


def on_device(
    token_qkv,
    text_kv,
    residual,
    query_gain,
    key_gain,
    out_weight,
    res_gate,
    mod_shift,
    mod_scale,
    final_weight,
    final_bias,
    text_len,
    video_frames,
    in_weight,
    in_bias,
    group_gain,
    group_bias,
    conv_weight,
    conv_bias,
):
    heads_dev = out_weight.shape[0]
    frames_dev = token_qkv.shape[1]
    patch_rows = token_qkv.shape[2]
    patches = patch_rows * lax.axis_size("seq")
    query_count = frames_dev * patches
    token_mix, text_mix = (
        lax.all_to_all(token_qkv, "seq", split_axis=4, concat_axis=2, tiled=True),
        lax.all_to_all(text_kv[:, None], "seq", split_axis=4, concat_axis=2, tiled=True),
    )
    token_mix = token_mix.reshape(query_count, 3, heads_dev, HD)
    text_mix = text_mix.reshape(TXT, 2, heads_dev, HD)
    query_rows = rms_scale(token_mix[:, 0], query_gain).astype(jnp.bfloat16)
    key_rows = rms_scale(token_mix[:, 1], key_gain).astype(jnp.bfloat16)
    value_rows = token_mix[:, 2]
    text_keys = rms_scale(text_mix[:, 0], key_gain).astype(jnp.bfloat16)
    text_values = text_mix[:, 1]
    frame_limit = video_frames[0]
    text_live = jnp.arange(TXT, dtype=jnp.int32) < text_len[0]
    text_scores = jnp.einsum(
        "qhd,khd->hqk", query_rows, text_keys, preferred_element_type=jnp.float32
    ) / math.sqrt(HD)
    text_scores = jnp.where(text_live[None, None, :], text_scores, -jnp.inf)
    running_max = jnp.max(text_scores, axis=-1)
    text_weights = jnp.exp(text_scores - running_max[:, :, None])
    running_sum = jnp.sum(text_weights, axis=-1)
    running_acc = jnp.einsum(
        "hqk,khd->hqd",
        text_weights.astype(jnp.bfloat16),
        text_values,
        preferred_element_type=jnp.float32,
    )
    piece_keys = lax.all_gather(key_rows, "frame", axis=0, tiled=True)
    piece_values = lax.all_gather(value_rows, "frame", axis=0, tiled=True)
    piece_len = piece_keys.shape[0]
    piece_scores = jnp.einsum(
        "qhd,khd->hqk", query_rows, piece_keys, preferred_element_type=jnp.float32
    ) / math.sqrt(HD)
    frame_index = jnp.arange(piece_len, dtype=jnp.int32) // patches
    piece_scores = jnp.where((frame_index < frame_limit)[None, None, :], piece_scores, -jnp.inf)
    max_next = jnp.maximum(running_max, jnp.max(piece_scores, axis=-1))
    rescale = jnp.exp(running_max - max_next)
    piece_weights = jnp.exp(piece_scores - max_next[:, :, None])
    sum_next = running_sum * rescale + jnp.sum(piece_weights, axis=-1)
    acc_next = running_acc * rescale[:, :, None] + jnp.einsum(
        "hqk,khd->hqd",
        piece_weights.astype(jnp.bfloat16),
        piece_values,
        preferred_element_type=jnp.float32,
    )
    attended = (acc_next / sum_next[:, :, None]).astype(jnp.bfloat16)
    attended = (
        attended.reshape(heads_dev, frames_dev, patches, HD)
        .transpose(2, 1, 0, 3)
        .reshape(patches, frames_dev, heads_dev * HD)
    )
    flat_out = out_weight.reshape(heads_dev * HD, -1)
    projected = (
        lax.psum_scatter(
            jnp.dot(attended, flat_out, preferred_element_type=jnp.float32).astype(jnp.bfloat16),
            "seq",
            scatter_dimension=0,
            tiled=True,
        )
        .astype(jnp.float32)
        .transpose(1, 0, 2)
    )
    block_sum = residual[0].astype(jnp.float32) + res_gate[0] * projected
    centred = block_sum - jnp.mean(block_sum, axis=-1, keepdims=True)
    variance = jnp.mean(centred * centred, axis=-1, keepdims=True)
    normed = centred * lax.rsqrt(variance + EPSILON)
    modulated = (normed * (1.0 + mod_scale[0]) + mod_shift[0]).astype(jnp.bfloat16)
    latent = lax.dot_general(
        modulated, final_weight, (((2,), (1,)), ((), ())), preferred_element_type=jnp.float32
    )
    latent = (latent + final_bias).astype(jnp.bfloat16)
    every_video = lax.all_gather(latent[None], "chan", axis=0, tiled=True)
    slab_latent = lax.all_to_all(every_video, "seq", split_axis=0, concat_axis=2, tiled=True)
    vids_dev = slab_latent.shape[0]
    volume = slab_latent.reshape(vids_dev, frames_dev, PH, PW, LCH, 2, 2).transpose(
        4, 0, 1, 2, 5, 3, 6
    )
    volume = volume.reshape(LCH, vids_dev, frames_dev, 2 * PH, 2 * PW)
    arrived = passed_along(volume, "frame", 1)
    chan_dev = in_weight.shape[2]
    cell_count = vids_dev * frames_dev * 4 * PH * PW
    hidden = (
        conv_taps(causal_edge(volume, arrived), in_weight, frames_dev) + in_bias[:, None]
    ).astype(jnp.bfloat16)
    group_size = DCH // GROUPS
    group_view = hidden.astype(jnp.float32).reshape(
        chan_dev // group_size, group_size, vids_dev, frames_dev, 4 * PH * PW
    )
    group_mean = jnp.mean(group_view, axis=(1, 4), keepdims=True)
    group_var = (
        jnp.mean(group_view * group_view, axis=(1, 4), keepdims=True) - group_mean * group_mean
    )
    normed_groups = (group_view - group_mean) * lax.rsqrt(group_var + EPSILON)
    normed_groups = normed_groups.reshape(chan_dev, cell_count)
    activated = jax.nn.silu(normed_groups * group_gain[:, None] + group_bias[:, None]).astype(
        jnp.bfloat16
    )
    activated = activated.reshape(chan_dev, vids_dev, frames_dev, 2 * PH, 2 * PW)
    arrived_act = passed_along(activated, "frame", 1)
    extended = causal_edge(activated, arrived_act)
    branch = conv_taps(
        lax.all_gather(extended, "chan", axis=0, tiled=True), conv_weight, frames_dev
    )
    decoded = (hidden.astype(jnp.float32) + branch + conv_bias[:, None]).astype(jnp.bfloat16)
    return decoded.reshape(chan_dev, vids_dev, frames_dev, 4 * PH * PW).transpose(1, 2, 0, 3)


def solution(mesh):
    return jax.shard_map(
        on_device,
        mesh=mesh,
        in_specs=(
            P("chan", "frame", "seq", None, None, None),
            P("chan", "seq", None, None, None),
            P("chan", "frame", "seq", None),
            P(),
            P(),
            P("seq", None, None),
            P("chan", None),
            P("chan", None),
            P("chan", None),
            P(),
            P(),
            P("chan"),
            P("chan"),
            P(None, None, "chan"),
            P("chan"),
            P("chan"),
            P("chan"),
            P(None, None, "chan"),
            P("chan"),
        ),
        out_specs=P("seq", "frame", "chan", None),
        check_vma=False,
    )
```

profile of v0, /device:TPU:9, one launch (start us, length us, event | category | flops | bytes accessed | tf_op | source)
XLA Modules:
  0.0 381.1 jit_solution(79900335427897971)
XLA Ops:
  6.5 1.9 copy.48
  8.4 10.0 %all-to-all-start = ((bf16[1,2,8,3,24,128]{5,2,3,1,0,4:T(8,128)(2,1)}), bf16[1,2,8,3,24,128]{5,2,3,1,0,4:T(8,128)(2,1)S(1)}, u32[]{:S(2)}, u32[]{:S(2)}) async-start(bf16[1,2,8,3,24,128]{5,2,3,1,0,4:T(8,128)(2,1)} %copy.48), calls=%async_computation | async-start | bytes 589824 | tf_op jit(solution)/shard_map/all_to_all | solution.py:87
  19.1 1.9 copy.70
  22.7 6.9 %all-to-all-done = bf16[1,2,8,3,24,128]{5,2,3,1,0,4:T(8,128)(2,1)S(1)} async-done(((bf16[1,2,8,3,24,128]{5,2,3,1,0,4:T(8,128)(2,1)}), bf16[1,2,8,3,24,128]{5,2,3,1,0,4:T(8,128)(2,1)S(1)}, u32[]{:S(2)}, u32[]{:S(2)}) %all-to-all-start) | async-done | bytes 294944 | tf_op jit(solution)/shard_map/all_to_all | solution.py:87
  29.6 4.1 %all-to-all-start.1 = ((bf16[1,1,32,2,24,128]{5,2,3,1,0,4:T(8,128)(2,1)}), bf16[1,1,32,2,24,128]{5,2,3,1,0,4:T(8,128)(2,1)}, u32[]{:S(2)}, u32[]{:S(2)}) async-start(bf16[1,1,32,2,24,128]{5,2,3,1,0,4:T(8,128)(2,1)} %bitcast.175), calls=%async_computation.1 | async-start | bytes 786432 | tf_op jit(solution)/shard_map/all_to_all | solution.py:88
  34.9 12.5 %all_gather.12 = bf16[512,3,128]{2,0,1:T(8,128)(2,1)S(1)} all-gather(bf16[128,3,128]{2,0,1:T(8,128)(2,1)S(1)} %fusion.31), channel_id=1, replica_groups=mesh['seq'=8,'chan'=16,'frame'=4] {'frame'}, dimensions={0}, use_global_device_ids=true | all-gather | bytes 491520 | tf_op jit(solution)/shard_map/all_gather | solution.py:112
  47.4 12.3 %all-gather = bf16[512,1,3,128]{3,0,2,1:T(8,128)(2,1)} all-gather(bf16[128,1,3,128]{3,0,2,1:T(8,128)(2,1)S(1)} %slice.248), channel_id=2, replica_groups=mesh['seq'=8,'chan'=16,'frame'=4] {'frame'}, dimensions={0}, use_global_device_ids=true | all-gather | bytes 491520 | tf_op jit(solution)/shard_map/all_gather | solution.py:113
  62.6 1.1 fusion.51
  64.6 1.3 fusion.6
  68.3 43.7 %reduce-scatter.4.cloned.1.call-done = bf16[8,6144]{1,0:T(8,128)(2,1)} async-done(((bf16[64,6144]{1,0:T(8,128)(2,1)}), bf16[8,6144]{1,0:T(8,128)(2,1)}) %reduce-scatter.4.cloned.1.call-update) | async-done | bytes 98320
  113.1 1.1 multiply_reduce_fusion
  114.2 1.4 fusion.13
  115.7 35.6 %all-gather.1 = bf16[32,8,64]{2,1,0:T(8,128)(2,1)S(1)} all-gather(bf16[2,8,64]{2,1,0:T(8,128)(2,1)S(1)} %fusion.13), channel_id=3, replica_groups=mesh['seq'=8,'chan'=16,'frame'=4] {'chan'}, dimensions={0}, use_global_device_ids=true | all-gather | bytes 34816 | tf_op jit(solution)/shard_map/all_gather | solution.py:156
  151.3 10.6 %all_to_all.45 = bf16[8,2,1024]{2,1,0:T(2,128)(2,1)S(1)} all-to-all(bf16[8,2,1024]{2,1,0:T(2,128)(2,1)S(1)} %reshape.394), channel_id=1, replica_groups=mesh['seq'=8,'chan'=16,'frame'=4] {'seq'}, dimensions={0} | all-to-all | bytes 65536 | tf_op jit(solution)/shard_map/all_to_all | solution.py:157
  163.0 2.2 collective-permute-start
  165.2 5.9 %collective-permute-done = bf16[16,2,2,8,32]{0,4,3,2,1:T(8,128)(2,1)S(1)} collective-permute-done((bf16[16,2,2,8,32]{0,4,3,2,1:T(8,128)(2,1)S(1)}, bf16[16,2,2,8,32]{0,4,3,2,1:T(8,128)(2,1)S(1)}, u32[]{:S(2)}, u32[]{:S(2)}) %collective-permute-start) | collective-permute-done | bytes 32800 | tf_op jit(solution)/shard_map/ppermute | solution.py:23
  171.3 2.9 pad_slice_fusion.24
  175.2 5.9 %concatenate.20 = bf16[432,1024]{0,1:T(8,128)(2,1)S(1)} concatenate(bf16[16,1024]{0,1:T(8,128)(2,1)} %bitcast.229, bf16[16,1024]{0,1:T(8,128)(2,1)} %bitcast.232, bf16[16,1024]{0,1:T(8,128)(2,1)} %bitcast.233, bf16[16,1024]{0,1:T(8,128)(2,1)} %bitcast.234, bf16[16,1024]{0,1:T(8,128)(2,1)S(1)} %bitcast.184, bf16[16,1024]{0,1:T(8,128)(2,1)} %bitcast.235, ...), dimensions={0} | concatenate | bytes 1769472 | tf_op jit(solution)/shard_map/concatenate | solution.py:46
  182.7 2.4 collective-permute-start.1
  185.0 4.7 %collective-permute-done.1 = bf16[32,2,2,8,32]{4,3,2,1,0:T(8,128)(2,1)S(1)} collective-permute-done((bf16[32,2,2,8,32]{4,3,2,1,0:T(8,128)(2,1)S(1)}, bf16[32,2,2,8,32]{4,3,2,1,0:T(8,128)(2,1)S(1)}, u32[]{:S(2)}, u32[]{:S(2)}) %collective-permute-start.1) | collective-permute-done | bytes 65568 | tf_op jit(solution)/shard_map/ppermute | solution.py:23
  190.8 2.2 copy.67
  193.0 103.9 %all-gather.4.cloned.1.call-done = bf16[512,2,4,8,32]{4,3,2,1,0:T(8,128)(2,1)} async-done(((bf16[32,2,4,8,32]{4,3,2,1,0:T(8,128)(2,1)}), bf16[512,2,4,8,32]{4,3,2,1,0:T(8,128)(2,1)}) %all-gather.4.cloned.1.call-update) | async-done | bytes 2097168 | tf_op jit(solution)/shard_map/all_gather | solution.py:186
  296.9 8.3 %copy.57 = bf16[512,2,4,8,32]{0,4,3,2,1:T(8,128)(2,1)S(1)} copy(bf16[512,2,4,8,32]{4,3,2,1,0:T(8,128)(2,1)} %all-gather.4.cloned.1.call-done) | data formatting | bytes 4194304 | tf_op jit(solution)/shard_map/all_gather | solution.py:186
  305.2 2.2 pad_slice_fusion.1
  307.4 8.6 %pad_slice_fusion = (bf16[512,2,2,8,32]{0,4,3,2,1:T(8,128)(2,1)}, bf16[512,2,2,8,32]{0,4,3,2,1:T(8,128)(2,1)}, bf16[512,2,2,8,32]{0,4,3,2,1:T(8,128)(2,1)}, bf16...) fusion(bf16[512,2,4,8,32]{0,4,3,2,1:T(8,128)(2,1)S(1)} %copy.57), kind=kLoop, calls=%fused_computation | loop fusion | bytes 22020096 | tf_op jit(solution)/shard_map/slice | solution.py:42
  317.1 3.1 constant_dynamic-update-slice_fusion.25
  320.2 2.3 constant_dynamic-update-slice_fusion.24
  322.5 2.3 constant_dynamic-update-slice_fusion.23
  324.8 1.1 constant_dynamic-update-slice_fusion.22
  326.0 2.3 constant_dynamic-update-slice_fusion.21
  328.3 2.4 constant_dynamic-update-slice_fusion.20
  330.7 2.3 constant_dynamic-update-slice_fusion.19
  333.0 2.3 constant_dynamic-update-slice_fusion.18
  335.3 2.3 constant_dynamic-update-slice_fusion.17
  337.6 2.3 constant_dynamic-update-slice_fusion.16
  340.0 2.4 constant_dynamic-update-slice_fusion.15
  342.4 2.3 constant_dynamic-update-slice_fusion.14
  345.7 1.2 constant_dynamic-update-slice_fusion.12
  346.9 1.1 constant_dynamic-update-slice_fusion.11
  348.0 1.2 constant_dynamic-update-slice_fusion.10
  351.3 1.1 constant_dynamic-update-slice_fusion.7
  352.4 1.1 constant_dynamic-update-slice_fusion.6
  353.5 1.1 constant_dynamic-update-slice_fusion.5
  354.6 1.1 constant_dynamic-update-slice_fusion.4
  355.7 1.1 constant_dynamic-update-slice_fusion.3
  357.9 1.1 constant_dynamic-update-slice_fusion.1
  359.0 1.1 constant_dynamic-update-slice_fusion
  360.1 13.5 %fusion.12 = bf16[32,1024]{1,0:T(8,128)(2,1)S(1)} fusion(f32[32,1024]{1,0:T(8,128)S(1)} %fusion.11, bf16[13824,1024]{0,1:T(8,128)(2,1)} %constant_dynamic-update-slice_fusion, bf16[13824,32]{0,1:T(8,128)(2,1)S(1)} %bitcast.212, f32[32]{0:T(128)S(1)} %copy-done.12), kind=kOutput, calls=%fused_computation.67 | convolution fusion | flops 906067968 | bytes 29393024 | tf_op jit(solution)/shard_map/dot_general | solution.py:48
  (94 shorter events, 20.2 us)
Async XLA Ops:
  6.5 59.4 %copy-start = (bf16[3,128,3072]{2,1,0:T(8,128)(2,1)S(1)}, bf16[3,128,3072]{2,1,0:T(8,128)(2,1)}, u32[]{:S(2)}) copy-start(bf16[3,128,3072]{2,1,0:T(8,128)(2,1)} %param.24) | copy-start | bytes 7077892
  6.5 174.6 %copy-start.11 = (bf16[27,16,32]{2,1,0:T(8,128)(2,1)S(1)}, bf16[27,16,32]{2,1,0:T(8,128)(2,1)}, u32[]{:S(2)}) copy-start(bf16[27,16,32]{2,1,0:T(8,128)(2,1)} %param.32) | copy-start | bytes 82948
  8.4 21.2 %all-to-all-start = ((bf16[1,2,8,3,24,128]{5,2,3,1,0,4:T(8,128)(2,1)}), bf16[1,2,8,3,24,128]{5,2,3,1,0,4:T(8,128)(2,1)S(1)}, u32[]{:S(2)}, u32[]{:S(2)}) async-start(bf16[1,2,8,3,24,128]{5,2,3,1,0,4:T(8,128)(2,1)} %copy.48), calls=%async_computation | async-start | bytes 589824 | tf_op jit(solution)/shard_map/all_to_all | solution.py:87
  29.6 31.8 %all-to-all-start.1 = ((bf16[1,1,32,2,24,128]{5,2,3,1,0,4:T(8,128)(2,1)}), bf16[1,1,32,2,24,128]{5,2,3,1,0,4:T(8,128)(2,1)}, u32[]{:S(2)}, u32[]{:S(2)}) async-start(bf16[1,1,32,2,24,128]{5,2,3,1,0,4:T(8,128)(2,1)} %bitcast.175), calls=%async_computation.1 | async-start | bytes 786432 | tf_op jit(solution)/shard_map/all_to_all | solution.py:88
  33.7 78.3 %reduce-scatter.4.cloned.1.call-start = ((), (), s32[]{:S(2)}) async-start(), calls=%async_computation.5 | async-start | bytes 884736
  59.7 0.6 copy-start.13
  63.8 117.4 %copy-start.14 = (f32[32]{0:T(128)S(1)}, f32[32]{0:T(128)}, u32[]{:S(2)}) copy-start(f32[32]{0:T(128)} %param.33) | copy-start | bytes 388
  63.8 118.5 %copy-start.15 = (f32[32]{0:T(128)S(1)}, f32[32]{0:T(128)}, u32[]{:S(2)}) copy-start(f32[32]{0:T(128)} %param.35) | copy-start | bytes 388
  63.8 118.5 %copy-start.16 = (f32[32]{0:T(128)S(1)}, f32[32]{0:T(128)}, u32[]{:S(2)}) copy-start(f32[32]{0:T(128)} %param.34) | copy-start | bytes 388
  67.5 229.4 %all-gather.4.cloned.1.call-start = ((), (), s32[]{:S(2)}) async-start(), calls=%async_computation.4 | async-start | bytes 8912896 | tf_op jit(solution)/shard_map/all_gather | solution.py:186
  163.0 8.1 %collective-permute-start = (bf16[16,2,2,8,32]{0,4,3,2,1:T(8,128)(2,1)S(1)}, bf16[16,2,2,8,32]{0,4,3,2,1:T(8,128)(2,1)S(1)}, u32[]{:S(2)}, u32[]{:S(2)}) collective-permute-start(bf16[16,2,2,8,32]{0,4,3,2,1:T(8,128)(2,1)S(1)} %bitcast.179), channel_id=1, source_target_pairs={{0,1},{1,2},{2,3},{4,5},{5,6},{6,7},{8,9},{9,10},{10,11},{12,13},{... | collective-permute-start | bytes 98312 | tf_op jit(solution)/shard_map/ppermute | solution.py:23
  182.7 7.1 %collective-permute-start.1 = (bf16[32,2,2,8,32]{4,3,2,1,0:T(8,128)(2,1)S(1)}, bf16[32,2,2,8,32]{4,3,2,1,0:T(8,128)(2,1)S(1)}, u32[]{:S(2)}, u32[]{:S(2)}) collective-permute-start(bf16[32,2,2,8,32]{4,3,2,1,0:T(8,128)(2,1)S(1)} %reshape.353), channel_id=1, source_target_pairs={{0,1},{1,2},{2,3},{4,5},{5,6},{6,7},{8,9},{9,10},{10,11},{12,13},{... | collective-permute-start | bytes 196616 | tf_op jit(solution)/shard_map/ppermute | solution.py:23
  315.9 29.8 %copy-start.9 = (bf16[512,2,2,8,32]{0,4,3,2,1:T(8,128)(2,1)S(1)}, bf16[512,2,2,8,32]{0,4,3,2,1:T(8,128)(2,1)}, u32[]{:S(2)}) copy-start(bf16[512,2,2,8,32]{0,4,3,2,1:T(8,128)(2,1)} %get-tuple-element.23) | copy-start | bytes 3145732
  316.0 31.0 %copy-start.8 = (bf16[512,2,2,8,32]{0,4,3,2,1:T(8,128)(2,1)S(1)}, bf16[512,2,2,8,32]{0,4,3,2,1:T(8,128)(2,1)}, u32[]{:S(2)}) copy-start(bf16[512,2,2,8,32]{0,4,3,2,1:T(8,128)(2,1)} %get-tuple-element.24) | copy-start | bytes 3145732
  316.0 32.1 %copy-start.7 = (bf16[512,2,2,8,32]{0,4,3,2,1:T(8,128)(2,1)S(1)}, bf16[512,2,2,8,32]{0,4,3,2,1:T(8,128)(2,1)}, u32[]{:S(2)}) copy-start(bf16[512,2,2,8,32]{0,4,3,2,1:T(8,128)(2,1)} %get-tuple-element.25) | copy-start | bytes 3145732
  316.0 33.2 %copy-start.6 = (bf16[512,2,2,8,32]{0,4,3,2,1:T(8,128)(2,1)S(1)}, bf16[512,2,2,8,32]{0,4,3,2,1:T(8,128)(2,1)}, u32[]{:S(2)}) copy-start(bf16[512,2,2,8,32]{0,4,3,2,1:T(8,128)(2,1)} %get-tuple-element.26) | copy-start | bytes 3145732
  316.0 34.3 %copy-start.5 = (bf16[512,2,2,8,32]{0,4,3,2,1:T(8,128)(2,1)S(1)}, bf16[512,2,2,8,32]{0,4,3,2,1:T(8,128)(2,1)}, u32[]{:S(2)}) copy-start(bf16[512,2,2,8,32]{0,4,3,2,1:T(8,128)(2,1)} %get-tuple-element.27) | copy-start | bytes 3145732
  316.0 35.3 %copy-start.4 = (bf16[512,2,2,8,32]{0,4,3,2,1:T(8,128)(2,1)S(1)}, bf16[512,2,2,8,32]{0,4,3,2,1:T(8,128)(2,1)}, u32[]{:S(2)}) copy-start(bf16[512,2,2,8,32]{0,4,3,2,1:T(8,128)(2,1)} %get-tuple-element.28) | copy-start | bytes 3145732
  316.0 36.4 %copy-start.3 = (bf16[512,2,2,8,32]{0,4,3,2,1:T(8,128)(2,1)S(1)}, bf16[512,2,2,8,32]{0,4,3,2,1:T(8,128)(2,1)}, u32[]{:S(2)}) copy-start(bf16[512,2,2,8,32]{0,4,3,2,1:T(8,128)(2,1)} %get-tuple-element.29) | copy-start | bytes 3145732
  316.0 43.0 %copy-start.2 = (bf16[512,2,2,8,32]{0,4,3,2,1:T(8,128)(2,1)S(1)}, bf16[512,2,2,8,32]{0,4,3,2,1:T(8,128)(2,1)}, u32[]{:S(2)}) copy-start(bf16[512,2,2,8,32]{0,4,3,2,1:T(8,128)(2,1)} %get-tuple-element.11) | copy-start | bytes 3145732
  316.0 44.1 %copy-start.10 = (bf16[27,4,8,512]{3,2,0,1:T(8,128)(2,1)S(1)}, bf16[27,4,8,512]{3,2,0,1:T(8,128)(2,1)}, u32[]{:S(2)}) copy-start(bf16[27,4,8,512]{3,2,0,1:T(8,128)(2,1)} %copy.67) | copy-start | bytes 2654212
  316.0 44.0 %copy-start.12 = (f32[32]{0:T(128)S(1)}, f32[32]{0:T(128)}, u32[]{:S(2)}) copy-start(f32[32]{0:T(128)} %param.37) | copy-start | bytes 388
  345.7 28.5 %copy-start.1 = (bf16[3,128,3072]{2,1,0:T(8,128)(2,1)S(1)}, bf16[3,128,3072]{2,1,0:T(8,128)(2,1)}, u32[]{:S(2)}) copy-start(bf16[3,128,3072]{2,1,0:T(8,128)(2,1)} %param.24) | copy-start | bytes 7077892
Sparse Core Ops, SparseCore 0:
  67.7 44.3 reduce-scatter.3
  190.9 105.9 all-gather.3
where the time goes:
time: 383 us; the launch traced here: 381 us
  waiting for transfers between devices  165 us (43%)
  local copies, waits for them, and re-layouts  84 us (22%)
  blocking collectives  71 us (19%)
  matrix products  19.6 us (5%)
  starting transfers between devices  18.7 us (5%)
  between operations  15.2 us (4%)
  other arithmetic  7.26 us (2%)
    all_gather x1, waiting for transfers between devices, on_device(): lax.all_gather(extended, 'chan', axis=0, tiled=True)  104 us
    unnamed x65, local copies, waits for them, and re-layouts  48.4 us
    unnamed x3, waiting for transfers between devices  43.8 us
    all_gather x1, blocking collectives, on_device(): every_video = lax.all_gather(latent[None], 'chan', axis=0, tiled=True)  35.6 us
    slice x4, local copies, waits for them, and re-layouts, conv_taps(): padded[:, :, step_t:step_t + frames_out, step_y:step_y + height, step_x:s...  14.6 us
    dot_general x2, matrix products, conv_taps(): lax.dot_general(flat_weight, stacked, (((0,), (0,)), ((), ())), preferred...  13.9 us
    all_gather x1, blocking collectives, on_device(): piece_keys = lax.all_gather(key_rows, 'frame', axis=0, tiled=True)  12.5 us
    all_gather x1, blocking collectives, on_device(): piece_values = lax.all_gather(value_rows, 'frame', axis=0, tiled=True)  12.3 us
  transfers between devices with their start and end apart: 6, of which 5 were waited for; matrix products, arithmetic and copies ran while one was open for 2% of the time, Pallas kernels for 0%

commit v1 on v0

v1 whole, which is shorter than its diff:
```python
import math

import jax
import jax.numpy as jnp
from jax import lax
from jax.experimental import pallas as pl
from jax.experimental.pallas import tpu as pltpu
from jax.sharding import PartitionSpec as P

HD = 128
TXT = 256
DCH = 512
GROUPS = 32
PW = 16
EPSILON = 1e-06

F32 = jnp.float32
BF16 = jnp.bfloat16
VMEM = pl.BlockSpec(memory_space=pltpu.VMEM)
SMEM = pl.BlockSpec(memory_space=pltpu.SMEM)
PARAMS = pltpu.CompilerParams(vmem_limit_bytes=48 * 1024 * 1024)


def normed_rows(values, row_gain):
    mean_square = jnp.mean(values * values, axis=-1, keepdims=True)
    return values * lax.rsqrt(mean_square + EPSILON) * row_gain


def pack_kernel(place, token_ref, text_ref, query_gain_ref, key_gain_ref, out_ref):
    query_gain = query_gain_ref[...]
    key_gain = key_gain_ref[...]
    token = token_ref[...].astype(F32).reshape(16, 3, 24, HD)
    text = text_ref[...].astype(F32).reshape(8, 2, 24, HD)
    token_rows = [
        jnp.swapaxes(normed_rows(token[:, 0], query_gain), 0, 1).astype(BF16),
        jnp.swapaxes(normed_rows(token[:, 1], key_gain), 0, 1).astype(BF16),
        jnp.swapaxes(token[:, 2], 0, 1).astype(BF16),
    ]
    text_keys = jnp.swapaxes(normed_rows(text[:, 0], key_gain), 0, 1)
    text_values = jnp.swapaxes(text[:, 1], 0, 1)
    text_rows = jnp.concatenate([text_keys, text_values], axis=1).astype(BF16)
    for seq in range(8):
        for head in range(3):
            source = 3 * seq + head
            target = 4 * seq + head
            for slot in range(3):
                out_ref[target, 16 * slot : 16 * slot + 16, :] = token_rows[slot][source]
            out_ref[target, 48:64, :] = text_rows[source]
        out_ref[4 * seq + 3] = jnp.zeros((64, HD), BF16)


def attend_kernel(limits, rows_ref, out_ref):
    keys = jnp.concatenate(
        [
            rows_ref[:, :, 16:32, :].reshape(512, HD),
            rows_ref[:, :, 48:64, :].astype(F32)[:, :, 0:8].reshape(TXT, HD).astype(BF16),
        ],
        axis=0,
    )
    values = jnp.concatenate(
        [
            rows_ref[:, :, 32:48, :].reshape(512, HD),
            rows_ref[:, :, 48:64, :].astype(F32)[:, :, 8:16].reshape(TXT, HD).astype(BF16),
        ],
        axis=0,
    )
    column = lax.broadcasted_iota(jnp.int32, (1, 512 + TXT), 1)
    position = jnp.where(column < 512, (column >> 3) & 7, column - 512)
    limit = jnp.where(column < 512, limits[0], limits[1])
    penalty = jnp.where(position < limit, 0.0, -jnp.inf)
    for frame in range(4):
        queries = rows_ref[:, frame, 0:16, :].reshape(128, HD)
        scores = lax.dot_general(
            queries, keys, (((1,), (1,)), ((), ())), preferred_element_type=F32
        ) * (1.0 / math.sqrt(HD))
        scores = scores + penalty
        weights = jnp.exp(scores - jnp.max(scores, axis=-1, keepdims=True))
        weight_sum = jnp.sum(weights, axis=-1, keepdims=True)
        attended = jnp.dot(weights.astype(BF16), values, preferred_element_type=F32)
        out_ref[frame] = (attended / weight_sum).astype(BF16)


def project_kernel(attended_ref, weight_ref, out_ref):
    attended = jnp.concatenate([attended_ref[0], attended_ref[1], attended_ref[2]], axis=1)
    for start in range(0, 3072, 512):
        weight = weight_ref[:, :, start : start + 512].reshape(3 * HD, 512)
        total = jnp.dot(attended, weight, preferred_element_type=F32)
        out_ref[:, :, start : start + 512] = total.astype(BF16).reshape(8, 16, 512)


def latent_kernel(
    place, parts_ref, residual_ref, gate_ref, shift_ref, scale_ref, weight_ref, bias_ref, out_ref
):
    projected = parts_ref[0].astype(F32)
    for source in range(1, 8):
        projected += parts_ref[source].astype(F32)
    block = residual_ref[...].astype(F32) + gate_ref[...] * projected
    centred = block - jnp.mean(block, axis=-1, keepdims=True)
    variance = jnp.mean(centred * centred, axis=-1, keepdims=True)
    normed = centred * lax.rsqrt(variance + EPSILON)
    modulated = (normed * (1.0 + scale_ref[...]) + shift_ref[...]).astype(BF16)
    latent = lax.dot_general(
        weight_ref[...], modulated, (((1,), (1,)), ((), ())), preferred_element_type=F32
    )
    latent = (latent + bias_ref[...]).astype(BF16)
    token = lax.broadcasted_iota(jnp.int32, (16, 128), 0)
    lane = lax.broadcasted_iota(jnp.int32, (16, 128), 1)
    local = ((lane >> 4) & 1) ^ (place[2] & 1)
    spread = jnp.where(token == local * 8 + ((lane & 15) >> 1), 1.0, 0.0).astype(BF16)
    wide = jnp.dot(latent, spread, preferred_element_type=F32)
    entry = lax.broadcasted_iota(jnp.int32, (64, 128), 0)
    lane = lax.broadcasted_iota(jnp.int32, (64, 128), 1)
    wanted = (lane >> 6) * 4 + ((lane >> 5) & 1) * 2 + (lane & 1)
    wide = jnp.where((entry >> 5) * 4 + (entry & 3) == wanted, wide, 0.0).astype(BF16)
    row = lax.broadcasted_iota(jnp.int32, (16, 64), 0)
    entry = lax.broadcasted_iota(jnp.int32, (16, 64), 1)
    pick = jnp.where(((entry >> 2) & 7) == (row & 7), 1.0, 0.0).astype(BF16)
    copies = jnp.dot(pick, wide, preferred_element_type=F32).astype(BF16)
    for pair in range(32):
        out_ref[16 * pair : 16 * pair + 16, :] = copies


def shifted(field, tap):
    step_y = tap // 3 - 1
    step_x = tap % 3 - 1
    offset = 32 * step_y + step_x
    if offset == 0:
        return field
    moved = pltpu.roll(field, (-offset) % 256, 1)
    pixel = lax.broadcasted_iota(jnp.int32, (1, 256), 1)
    row = (pixel >> 5) + step_y
    col = (pixel & 31) + step_x
    inside = (row >= 0) & (row < 8) & (col >= 0) & (col < 32)
    return jnp.where(inside, moved, 0.0)


def decode_kernel(
    place,
    latent_ref,
    in_weight_ref,
    columns_ref,
    weight_ref,
    bias_ref,
    out_ref,
    latent_scratch,
    taps_ref,
    hidden_ref,
    active_ref,
):
    chan = place[0]
    frame = place[1]
    in_bias = columns_ref[:, 48:49]
    gain = columns_ref[:, 49:50]
    bias = columns_ref[:, 50:51]
    latent_scratch[...] = latent_ref[...].astype(F32).reshape(64, 8, 128)
    lane = lax.broadcasted_iota(jnp.int32, (1, 128), 1)
    low = lane < 64
    even = (lane & 16) == 0
    for video in range(2):
        fields = []
        for step in range(3):
            slab = frame - 2 + step
            held = jnp.maximum(slab, 0)
            frames = ([], [])
            for row in range(4):
                left = latent_scratch[(4 * row + video) * 4 + held]
                right = latent_scratch[(4 * row + 2 + video) * 4 + held]
                frames[0].append(jnp.where(even, left, right))
                crossed = jnp.where(even, right, left)
                crossed = jnp.where(
                    even, pltpu.roll(crossed, 112, 1), pltpu.roll(crossed, 16, 1)
                )
                frames[1].append(crossed)
            made = []
            for rows in frames:
                turned = [pltpu.roll(piece, 64, 1) for piece in rows]
                upper = [jnp.where(low, rows[0], turned[1]), jnp.where(low, rows[2], turned[3])]
                lower = [jnp.where(low, turned[0], rows[1]), jnp.where(low, turned[2], rows[3])]
                made.append(
                    jnp.concatenate(
                        [jnp.concatenate(upper, axis=1), jnp.concatenate(lower, axis=1)], axis=0
                    )
                )
            fields += [made[0], jnp.where(slab < 0, made[0], made[1])]
        stacked = jnp.concatenate(fields, axis=0)
        for tap in range(9):
            moved = shifted(stacked, tap)
            for step in range(6):
                taps_ref[9 * step + tap] = moved[16 * step : 16 * step + 16]
        taps_ref[54:59] = jnp.zeros((5, 16, 256), F32)
        for step in range(4):
            window = taps_ref[9 * step : 9 * step + 32].reshape(DCH, 256).astype(BF16)
            hidden = jnp.dot(in_weight_ref[...], window, preferred_element_type=F32) + in_bias
            hidden = hidden.astype(BF16).astype(F32)
            if step >= 2:
                hidden_ref[step - 2] = hidden.reshape(16, 32, 256)
            halves = hidden[:, :128] + hidden[:, 128:]
            total = jnp.sum(halves.reshape(GROUPS, 16, 128), axis=1)
            mean = jnp.sum(total, axis=1, keepdims=True) * (1.0 / 4096.0)
            square = hidden * hidden
            halves = square[:, :128] + square[:, 128:]
            total = jnp.sum(halves.reshape(GROUPS, 16, 128), axis=1)
            variance = jnp.sum(total, axis=1, keepdims=True) * (1.0 / 4096.0) - mean * mean
            inverse = lax.rsqrt(variance + EPSILON)
            mean = jnp.broadcast_to(mean[:, None, :], (GROUPS, 16, 1)).reshape(DCH, 1)
            inverse = jnp.broadcast_to(inverse[:, None, :], (GROUPS, 16, 1)).reshape(DCH, 1)
            normed = (hidden - mean) * (inverse * gain) + bias
            active = 0.5 * normed * (1.0 + jnp.tanh(0.5 * normed))
            active_ref[step] = active
        for step in range(2):
            branch = jnp.zeros((288, 256), F32)
            for lag in range(3):
                branch += jnp.dot(
                    weight_ref[9 * lag : 9 * lag + 9].reshape(288, DCH),
                    active_ref[step + lag].astype(BF16),
                    preferred_element_type=F32,
                )
            total = hidden_ref[step, chan] + bias_ref[...]
            for tap in range(9):
                total += shifted(branch[32 * tap : 32 * tap + 32], tap)
            out_ref[video, step] = total.astype(BF16)


def on_device(
    token_qkv,
    text_kv,
    residual,
    query_gain,
    key_gain,
    out_weight,
    res_gate,
    mod_shift,
    mod_scale,
    final_weight,
    final_bias,
    text_len,
    video_frames,
    in_weight,
    in_bias,
    group_gain,
    group_bias,
    conv_weight,
    conv_bias,
):
    place = jnp.stack(
        [lax.axis_index("chan"), lax.axis_index("frame"), lax.axis_index("seq")]
    ).astype(jnp.int32)
    limits = jnp.concatenate([video_frames, text_len])

    table = jnp.concatenate(
        [
            in_weight.reshape(432, 32).T.astype(F32),
            in_bias[:, None],
            group_gain[:, None],
            group_bias[:, None],
            jnp.zeros((32, 77), F32),
        ],
        axis=1,
    )
    table = lax.all_gather(table, "chan", axis=0, tiled=True)
    lane = jnp.arange(512)[None]
    in_rows = jnp.where(lane < 432, table, 0.0).astype(BF16)
    columns = table[:, 384:]

    packed = pl.pallas_call(
        pack_kernel,
        out_shape=jax.ShapeDtypeStruct((32, 64, HD), BF16),
        grid_spec=pltpu.PrefetchScalarGridSpec(
            num_scalar_prefetch=1,
            grid=(1,),
            in_specs=[
                pl.BlockSpec((1152, HD), lambda i, p: (0, 0)),
                pl.BlockSpec((384, HD), lambda i, p: (p[1], 0)),
                pl.BlockSpec((1, HD), lambda i, p: (0, 0)),
                pl.BlockSpec((1, HD), lambda i, p: (0, 0)),
            ],
            out_specs=pl.BlockSpec((32, 64, HD), lambda i, p: (0, 0, 0)),
        ),
        compiler_params=pltpu.CompilerParams(vmem_limit_bytes=62 * 1024 * 1024),
        name="pack_rows",
    )(
        place,
        token_qkv.reshape(1152, HD),
        text_kv.reshape(1536, HD),
        query_gain[None],
        key_gain[None],
    )
    rows = lax.all_to_all(packed, ("seq", "frame"), 0, 0, tiled=True)
    attended = pl.pallas_call(
        attend_kernel,
        out_shape=jax.ShapeDtypeStruct((4, 128, HD), BF16),
        in_specs=[SMEM, VMEM],
        out_specs=VMEM,
        compiler_params=PARAMS,
        name="attend",
    )(limits, rows.reshape(8, 4, 64, HD))
    attended = lax.all_to_all(attended, "frame", 0, 0, tiled=True)
    parts = pl.pallas_call(
        project_kernel,
        out_shape=jax.ShapeDtypeStruct((8, 16, 3072), BF16),
        in_specs=[VMEM, VMEM],
        out_specs=VMEM,
        compiler_params=PARAMS,
        name="project",
    )(attended, out_weight)
    parts = lax.all_to_all(parts, "seq", 0, 0, tiled=True)
    latent = pl.pallas_call(
        latent_kernel,
        out_shape=jax.ShapeDtypeStruct((512, 128), BF16),
        in_specs=[SMEM] + [VMEM] * 7,
        out_specs=VMEM,
        compiler_params=PARAMS,
        name="latents",
    )(
        place,
        parts,
        residual.reshape(16, 3072),
        res_gate,
        mod_shift,
        mod_scale,
        final_weight,
        final_bias[:, None],
    )
    latent = lax.all_to_all(latent.reshape(64, 8, 128), ("chan", "frame"), 0, 0, tiled=True)
    latent = lax.all_to_all(latent, "seq", 0, 0, tiled=True)
    return pl.pallas_call(
        decode_kernel,
        out_shape=jax.ShapeDtypeStruct((2, 2, 32, 256), BF16),
        in_specs=[SMEM] + [VMEM] * 5,
        out_specs=VMEM,
        scratch_shapes=[
            pltpu.VMEM((64, 8, 128), F32),
            pltpu.VMEM((59, 16, 256), F32),
            pltpu.VMEM((2, 16, 32, 256), F32),
            pltpu.VMEM((4, DCH, 256), F32),
        ],
        compiler_params=PARAMS,
        name="decode",
    )(
        place,
        latent.reshape(512, 128),
        in_rows,
        columns,
        conv_weight.transpose(0, 2, 1),
        conv_bias[:, None],
    )


def solution(mesh):
    return jax.shard_map(
        on_device,
        mesh=mesh,
        in_specs=(
            P("chan", "frame", "seq", None, None, None),
            P("chan", "seq", None, None, None),
            P("chan", "frame", "seq", None),
            P(),
            P(),
            P("seq", None, None),
            P("chan", None),
            P("chan", None),
            P("chan", None),
            P(),
            P(),
            P("chan"),
            P("chan"),
            P(None, None, "chan"),
            P("chan"),
            P("chan"),
            P("chan"),
            P(None, None, "chan"),
            P("chan"),
        ),
        out_specs=P("seq", "frame", "chan", None),
        check_vma=False,
    )
```

time: 383 us -> 127 us (0.33)
  the two profiles are of different devices: /device:TPU:9 before, /device:TPU:2 now
where the time goes in v1:
time: 127 us; the launch traced here: 126 us
  waiting for transfers between devices  52.5 us (41%)
  starting transfers between devices  31 us (24%)
  between operations  14.9 us (12%)
  Pallas kernels  13.5 us (11%)
  blocking collectives  10 us (8%)
  local copies, waits for them, and re-layouts  2.3 us (2%)
  other arithmetic  2.11 us (2%)
    all_to_all x1, waiting for transfers between devices, on_device(): parts = lax.all_to_all(parts, 'seq', 0, 0, tiled=True)  21 us
    all_to_all x1, waiting for transfers between devices, on_device(): rows = lax.all_to_all(packed, ('seq', 'frame'), 0, 0, tiled=True)  14.6 us
    all_to_all x1, starting transfers between devices, on_device(): rows = lax.all_to_all(packed, ('seq', 'frame'), 0, 0, tiled=True)  13.9 us
    all_to_all x1, blocking collectives, on_device(): attended = lax.all_to_all(attended, 'frame', 0, 0, tiled=True)  10 us
    all_to_all x1, starting transfers between devices, on_device(): lax.all_to_all(latent.reshape(64, 8, 128), ('chan', 'frame'), 0, 0, tiled...  10 us
    all_to_all x1, waiting for transfers between devices, on_device(): lax.all_to_all(latent.reshape(64, 8, 128), ('chan', 'frame'), 0, 0, tiled...  9.25 us
    all_to_all x1, waiting for transfers between devices, on_device(): latent = lax.all_to_all(latent, 'seq', 0, 0, tiled=True)  7.65 us
    pallas_call x1, Pallas kernels, on_device(): pl.pallas_call(decode_kernel, out_shape=jax.ShapeDtypeStruct((2, 2, 32, 2...  5.33 us
  transfers between devices with their start and end apart: 5, of which 4 were waited for; matrix products, arithmetic and copies ran while one was open for 3% of the time, Pallas kernels for 4%

profile of v1, /device:TPU:2, one launch (start us, length us, event | category | flops | bytes accessed | tf_op | source)
XLA Modules:
  0.0 126.3 jit_solution(8107679429741406583)
XLA Ops:
  6.5 0.0 copy-start.8
  6.5 0.7 pad_add_fusion.place
  7.2 2.7 %pack_rows.1 = bf16[32,64,128]{2,1,0:T(8,128)(2,1)} custom-call(s32[3]{0:T(128)} %pad_add_fusion.place, bf16[1152,128]{1,0:T(8,128)(2,1)} %bitcast.26, bf16[1536,128]{1,0:T(8,128)(2,1)} %bitcast.25, f32[1,128]{1,0:T(1,128)} %bitcast.28, f32[1,128]{1,0:T(1,128)} %bitcast.29), custom_call_target="tpu_custom_call" | custom-call | tf_op jit(solution)/shard_map/pack_rows/pallas_call | solution.py:265
  9.9 13.9 %all-to-all-start = ((bf16[32,64,128]{2,1,0:T(8,128)(2,1)}), bf16[32,64,128]{2,1,0:T(8,128)(2,1)S(1)}, u32[]{:S(2)}, u32[]{:S(2)}) async-start(bf16[32,64,128]{2,1,0:T(8,128)(2,1)} %pack_rows.1), calls=%async_computation | async-start | bytes 1048576 | tf_op jit(solution)/shard_map/all_to_all | solution.py:288
  23.8 0.0 all-gather.2.cloned.1.call-start
  23.9 0.0 copy-done.8
  23.9 0.1 copy.27
  24.0 0.0 copy-done.10
  24.0 0.1 copy.28
  24.1 0.0 copy-done.11
  24.1 0.1 copy.29
  24.2 0.0 copy-done.12
  24.2 0.1 copy.30
  24.3 0.7 concatenate.7
  25.0 0.0 all-gather.2.cloned.1.call-update
  26.3 0.1 pad_add_fusion.1.limits
  26.4 14.6 %all-to-all-done = bf16[32,64,128]{2,1,0:T(8,128)(2,1)S(1)} async-done(((bf16[32,64,128]{2,1,0:T(8,128)(2,1)}), bf16[32,64,128]{2,1,0:T(8,128)(2,1)S(1)}, u32[]{:S(2)}, u32[]{:S(2)}) %all-to-all-start) | async-done | bytes 524320 | tf_op jit(solution)/shard_map/all_to_all | solution.py:288
  41.0 2.0 %attend.1 = bf16[4,128,128]{2,1,0:T(8,128)(2,1)S(1)} custom-call(s32[2]{0:T(128)S(1)} %pad_add_fusion.1.limits, bf16[8,4,64,128]{3,2,1,0:T(8,128)(2,1)S(1)} %bitcast.21), custom_call_target="tpu_custom_call" | custom-call | tf_op jit(solution)/shard_map/attend/pallas_call | solution.py:289
  43.0 10.0 %all_to_all.25.attended_ref = bf16[4,128,128]{2,1,0:T(8,128)(2,1)S(1)} all-to-all(bf16[4,128,128]{2,1,0:T(8,128)(2,1)S(1)} %attend.1), channel_id=1, replica_groups=mesh['seq'=8,'chan'=16,'frame'=4] {'frame'}, dimensions={0} | all-to-all | bytes 262144 | tf_op jit(solution)/shard_map/all_to_all | solution.py:297
  53.0 0.0 copy-done
  53.1 0.0 copy-start.4
  53.1 0.0 copy-start.5
  53.1 0.0 copy-start.6
  53.1 0.0 copy-start.7
  53.1 1.5 %project.1 = bf16[8,16,3072]{2,1,0:T(8,128)(2,1)} custom-call(bf16[4,128,128]{2,1,0:T(8,128)(2,1)S(1)} %all_to_all.25.attended_ref, bf16[3,128,3072]{2,1,0:T(8,128)(2,1)S(1)} %copy-done), custom_call_target="tpu_custom_call" | custom-call | tf_op jit(solution)/shard_map/project/pallas_call | solution.py:298
  54.6 3.7 %all-to-all-start.2 = ((bf16[8,16,3072]{2,1,0:T(8,128)(2,1)}), bf16[8,16,3072]{2,1,0:T(8,128)(2,1)S(1)}, u32[]{:S(2)}, u32[]{:S(2)}) async-start(bf16[8,16,3072]{2,1,0:T(8,128)(2,1)} %project.1), calls=%async_computation.2 | async-start | bytes 1572864 | tf_op jit(solution)/shard_map/all_to_all | solution.py:306
  58.3 0.0 copy-start.1
  58.3 0.0 copy-done.9
  58.3 0.1 copy.26.bias_ref
  58.4 21.0 %all-to-all-done.2.parts_ref = bf16[8,16,3072]{2,1,0:T(8,128)(2,1)S(1)} async-done(((bf16[8,16,3072]{2,1,0:T(8,128)(2,1)}), bf16[8,16,3072]{2,1,0:T(8,128)(2,1)S(1)}, u32[]{:S(2)}, u32[]{:S(2)}) %all-to-all-start.2) | async-done | bytes 786464 | tf_op jit(solution)/shard_map/all_to_all | solution.py:306
  79.4 0.0 copy-done.2
  79.4 0.0 copy-done.3
  79.4 0.0 copy-done.4
  79.4 0.0 copy-done.5
  79.4 0.0 copy-done.6
  79.4 0.0 copy-done.7
  79.4 2.0 %latents.1 = bf16[512,128]{1,0:T(8,128)(2,1)} custom-call(s32[3]{0:T(128)S(1)} %copy-done.7, bf16[8,16,3072]{2,1,0:T(8,128)(2,1)S(1)} %all-to-all-done.2.parts_ref, bf16[16,3072]{1,0:T(8,128)(2,1)S(1)} %bitcast.24, f32[1,3072]{1,0:T(1,128)S(1)} %copy-done.4, f32[1,3072]{1,0:T(1,128)S(1)} %copy-done.5, f32[1,3072]{1,0:T(1,128)S(1)} %copy-done.6, ...), custom_call_target="tpu_custom_call" | custom-call | tf_op jit(solution)/shard_map/latents/pallas_call | solution.py:307
  81.4 10.0 %all-to-all-start.3 = ((bf16[64,8,128]{2,1,0:T(8,128)(2,1)}), bf16[64,8,128]{2,1,0:T(8,128)(2,1)}, u32[]{:S(2)}, u32[]{:S(2)}) async-start(bf16[64,8,128]{2,1,0:T(8,128)(2,1)} %bitcast.10), calls=%async_computation.3 | async-start | bytes 262144 | tf_op jit(solution)/shard_map/all_to_all | solution.py:324
  91.4 0.0 copy-done.13
  91.4 0.1 copy.31.bias_ref
  91.5 0.0 all-gather.2.cloned.1.call-done
  91.5 1.0 slice.4.columns_ref
  92.5 9.2 %all-to-all-done.3 = bf16[64,8,128]{2,1,0:T(8,128)(2,1)} async-done(((bf16[64,8,128]{2,1,0:T(8,128)(2,1)}), bf16[64,8,128]{2,1,0:T(8,128)(2,1)}, u32[]{:S(2)}, u32[]{:S(2)}) %all-to-all-start.3) | async-done | bytes 131104 | tf_op jit(solution)/shard_map/all_to_all | solution.py:324
  101.8 3.4 %all-to-all-start.4 = ((bf16[64,8,128]{2,1,0:T(8,128)(2,1)}), bf16[64,8,128]{2,1,0:T(8,128)(2,1)S(1)}, u32[]{:S(2)}, u32[]{:S(2)}) async-start(bf16[64,8,128]{2,1,0:T(8,128)(2,1)} %all-to-all-done.3), calls=%async_computation.4 | async-start | bytes 262144 | tf_op jit(solution)/shard_map/all_to_all | solution.py:325
  105.1 1.3 %select_convert_fusion.in_weight_ref = bf16[512,512]{1,0:T(8,128)(2,1)S(1)} fusion(f32[512,512]{1,0:T(8,128)} %all-gather.2.cloned.1.call-done, pred[512]{0:T(512)(128)(4,1)S(1)} %iota_compare_fusion), kind=kLoop, calls=%fused_computation | loop fusion | flops 262144 | bytes 1573376 | tf_op jit(solution)/shard_map/convert_element_type | solution.py:262
  106.5 7.6 %all-to-all-done.4 = bf16[64,8,128]{2,1,0:T(8,128)(2,1)S(1)} async-done(((bf16[64,8,128]{2,1,0:T(8,128)(2,1)}), bf16[64,8,128]{2,1,0:T(8,128)(2,1)S(1)}, u32[]{:S(2)}, u32[]{:S(2)}) %all-to-all-start.4) | async-done | bytes 131104 | tf_op jit(solution)/shard_map/all_to_all | solution.py:325
  114.1 0.0 copy-done.1
  114.1 5.3 %decode.1 = bf16[2,2,32,256]{3,2,1,0:T(8,128)(2,1)} custom-call(s32[3]{0:T(128)S(1)} %copy-done.7, bf16[512,128]{1,0:T(8,128)(2,1)S(1)} %bitcast.23, bf16[512,512]{1,0:T(8,128)(2,1)S(1)} %select_convert_fusion.in_weight_ref, f32[512,128]{1,0:T(8,128)S(1)} %slice.4.columns_ref, bf16[27,32,512]{2,1,0:T(8,128)(2,1)S(1)} %bitcast.22, f32[32,1]{1,0:T(8,128)S(1)} %copy.31.bias_ref), custom_call_target="tpu_custom_call" | custom-call | tf_op jit(solution)/shard_map/decode/pallas_call | solution.py:326
  (11 shorter events, 0.0 us)
Async XLA Ops:
  6.5 17.3 %copy-start.8 = (bf16[27,16,32]{2,1,0:T(8,128)(2,1)S(1)}, bf16[27,16,32]{2,1,0:T(8,128)(2,1)}, u32[]{:S(2)}) copy-start(bf16[27,16,32]{2,1,0:T(8,128)(2,1)} %param.32) | copy-start | bytes 82948
  6.5 17.5 %copy-start.10 = (f32[32]{0:T(128)S(1)}, f32[32]{0:T(128)}, u32[]{:S(2)}) copy-start(f32[32]{0:T(128)} %param.33) | copy-start | bytes 388
  6.5 17.6 %copy-start.11 = (f32[32]{0:T(128)S(1)}, f32[32]{0:T(128)}, u32[]{:S(2)}) copy-start(f32[32]{0:T(128)} %param.34) | copy-start | bytes 388
  6.5 17.7 %copy-start.12 = (f32[32]{0:T(128)S(1)}, f32[32]{0:T(128)}, u32[]{:S(2)}) copy-start(f32[32]{0:T(128)} %param.35) | copy-start | bytes 388
  9.9 43.1 %copy-start = (bf16[3,128,3072]{2,1,0:T(8,128)(2,1)S(1)}, bf16[3,128,3072]{2,1,0:T(8,128)(2,1)}, u32[]{:S(2)}) copy-start(bf16[3,128,3072]{2,1,0:T(8,128)(2,1)} %weight_ref.2) | copy-start | bytes 7077892
  9.9 31.1 %all-to-all-start = ((bf16[32,64,128]{2,1,0:T(8,128)(2,1)}), bf16[32,64,128]{2,1,0:T(8,128)(2,1)S(1)}, u32[]{:S(2)}, u32[]{:S(2)}) async-start(bf16[32,64,128]{2,1,0:T(8,128)(2,1)} %pack_rows.1), calls=%async_computation | async-start | bytes 1048576 | tf_op jit(solution)/shard_map/all_to_all | solution.py:288
  23.8 67.7 %all-gather.2.cloned.1.call-start = ((), (), s32[]{:S(2)}) async-start(), calls=%async_computation.5 | async-start | bytes 1114112 | tf_op jit(solution)/shard_map/all_gather | solution.py:260
  53.0 5.2 %copy-start.9 = (f32[64]{0:T(128)S(1)}, f32[64]{0:T(128)}, u32[]{:S(2)}) copy-start(f32[64]{0:T(128)} %param.29) | copy-start | bytes 772
  53.0 26.3 %copy-start.2 = (bf16[64,3072]{1,0:T(8,128)(2,1)S(1)}, bf16[64,3072]{1,0:T(8,128)(2,1)}, u32[]{:S(2)}) copy-start(bf16[64,3072]{1,0:T(8,128)(2,1)} %weight_ref.3) | copy-start | bytes 1179652
  53.0 26.3 %copy-start.3 = (bf16[1,2,8,3072]{3,2,1,0:T(8,128)(2,1)S(1)}, bf16[1,2,8,3072]{3,2,1,0:T(8,128)(2,1)}, u32[]{:S(2)}) copy-start(bf16[1,2,8,3072]{3,2,1,0:T(8,128)(2,1)} %param.21) | copy-start | bytes 294916
  53.1 26.3 %copy-start.4 = (f32[1,3072]{1,0:T(1,128)S(1)}, f32[1,3072]{1,0:T(1,128)}, u32[]{:S(2)}) copy-start(f32[1,3072]{1,0:T(1,128)} %gate_ref.1) | copy-start | bytes 36868
  53.1 26.3 %copy-start.5 = (f32[1,3072]{1,0:T(1,128)S(1)}, f32[1,3072]{1,0:T(1,128)}, u32[]{:S(2)}) copy-start(f32[1,3072]{1,0:T(1,128)} %shift_ref.1) | copy-start | bytes 36868
  53.1 26.3 %copy-start.6 = (f32[1,3072]{1,0:T(1,128)S(1)}, f32[1,3072]{1,0:T(1,128)}, u32[]{:S(2)}) copy-start(f32[1,3072]{1,0:T(1,128)} %scale_ref.1) | copy-start | bytes 36868
  53.1 26.3 %copy-start.7 = (s32[3]{0:T(128)S(1)}, s32[3]{0:T(128)}, u32[]{:S(2)}) copy-start(s32[3]{0:T(128)} %pad_add_fusion.place) | copy-start | bytes 40
  54.6 36.8 %copy-start.13 = (f32[32]{0:T(128)S(1)}, f32[32]{0:T(128)}, u32[]{:S(2)}) copy-start(f32[32]{0:T(128)} %param.37) | copy-start | bytes 388
  54.6 24.8 %all-to-all-start.2 = ((bf16[8,16,3072]{2,1,0:T(8,128)(2,1)}), bf16[8,16,3072]{2,1,0:T(8,128)(2,1)S(1)}, u32[]{:S(2)}, u32[]{:S(2)}) async-start(bf16[8,16,3072]{2,1,0:T(8,128)(2,1)} %project.1), calls=%async_computation.2 | async-start | bytes 1572864 | tf_op jit(solution)/shard_map/all_to_all | solution.py:306
  58.3 55.9 %copy-start.1 = (bf16[27,512,32]{1,2,0:T(8,128)(2,1)S(1)}, bf16[27,512,32]{1,2,0:T(8,128)(2,1)}, u32[]{:S(2)}) copy-start(bf16[27,512,32]{1,2,0:T(8,128)(2,1)} %param.36) | copy-start | bytes 2654212
  81.4 20.4 %all-to-all-start.3 = ((bf16[64,8,128]{2,1,0:T(8,128)(2,1)}), bf16[64,8,128]{2,1,0:T(8,128)(2,1)}, u32[]{:S(2)}, u32[]{:S(2)}) async-start(bf16[64,8,128]{2,1,0:T(8,128)(2,1)} %bitcast.10), calls=%async_computation.3 | async-start | bytes 262144 | tf_op jit(solution)/shard_map/all_to_all | solution.py:324
  101.8 12.4 %all-to-all-start.4 = ((bf16[64,8,128]{2,1,0:T(8,128)(2,1)}), bf16[64,8,128]{2,1,0:T(8,128)(2,1)S(1)}, u32[]{:S(2)}, u32[]{:S(2)}) async-start(bf16[64,8,128]{2,1,0:T(8,128)(2,1)} %all-to-all-done.3), calls=%async_computation.4 | async-start | bytes 262144 | tf_op jit(solution)/shard_map/all_to_all | solution.py:325
Sparse Core Ops, SparseCore 0:
  28.0 57.1 all-gather.1

commit v2 on v1

--- a/solution.py
+++ b/solution.py
@@ -26,7 +26,7 @@
     return values * lax.rsqrt(mean_square + EPSILON) * row_gain
 
 
-def pack_kernel(place, token_ref, text_ref, query_gain_ref, key_gain_ref, out_ref):
+def pack_kernel(token_ref, text_ref, query_gain_ref, key_gain_ref, out_ref):
     query_gain = query_gain_ref[...]
     key_gain = key_gain_ref[...]
     token = token_ref[...].astype(F32).reshape(16, 3, 24, HD)
@@ -137,21 +137,29 @@
 def decode_kernel(
     place,
     latent_ref,
-    in_weight_ref,
-    columns_ref,
+    table_ref,
     weight_ref,
     bias_ref,
     out_ref,
     latent_scratch,
+    table_scratch,
     taps_ref,
     hidden_ref,
-    active_ref,
 ):
     chan = place[0]
     frame = place[1]
-    in_bias = columns_ref[:, 48:49]
-    gain = columns_ref[:, 49:50]
-    bias = columns_ref[:, 50:51]
+    def position(v):
+        return ((v >> 3) & 1) | ((v & 1) << 1) | (v & 4) | ((v & 2) << 2)
+
+    table_scratch[...] = table_ref[...].astype(F32)
+    table = jnp.concatenate(
+        [table_scratch[position(chan) ^ position(group)] for group in range(16)], axis=0
+    )
+    in_weight = table[:, :448].astype(BF16)
+    gain = 0.5 * (table[:, 435:436] + table[:, 436:437] + table[:, 437:438])
+    bias = 0.5 * (table[:, 438:439] + table[:, 439:440] + table[:, 440:441])
+    row = lax.broadcasted_iota(jnp.int32, (16, 256), 0)
+    ones = jnp.where(row < 3, 1.0, 0.0)
     latent_scratch[...] = latent_ref[...].astype(F32).reshape(64, 8, 128)
     lane = lax.broadcasted_iota(jnp.int32, (1, 128), 1)
     low = lane < 64
@@ -187,10 +195,11 @@
             moved = shifted(stacked, tap)
             for step in range(6):
                 taps_ref[9 * step + tap] = moved[16 * step : 16 * step + 16]
-        taps_ref[54:59] = jnp.zeros((5, 16, 256), F32)
+        active = []
         for step in range(4):
-            window = taps_ref[9 * step : 9 * step + 32].reshape(DCH, 256).astype(BF16)
-            hidden = jnp.dot(in_weight_ref[...], window, preferred_element_type=F32) + in_bias
+            window = taps_ref[9 * step : 9 * step + 27].reshape(432, 256)
+            window = jnp.concatenate([window, ones], axis=0).astype(BF16)
+            hidden = jnp.dot(in_weight, window, preferred_element_type=F32)
             hidden = hidden.astype(BF16).astype(F32)
             if step >= 2:
                 hidden_ref[step - 2] = hidden.reshape(16, 32, 256)
@@ -205,14 +214,13 @@
             mean = jnp.broadcast_to(mean[:, None, :], (GROUPS, 16, 1)).reshape(DCH, 1)
             inverse = jnp.broadcast_to(inverse[:, None, :], (GROUPS, 16, 1)).reshape(DCH, 1)
             normed = (hidden - mean) * (inverse * gain) + bias
-            active = 0.5 * normed * (1.0 + jnp.tanh(0.5 * normed))
-            active_ref[step] = active
+            active.append((normed + normed * jnp.tanh(normed)).astype(BF16))
         for step in range(2):
             branch = jnp.zeros((288, 256), F32)
             for lag in range(3):
                 branch += jnp.dot(
                     weight_ref[9 * lag : 9 * lag + 9].reshape(288, DCH),
-                    active_ref[step + lag].astype(BF16),
+                    active[step + lag],
                     preferred_element_type=F32,
                 )
             total = hidden_ref[step, chan] + bias_ref[...]
@@ -247,45 +255,43 @@
     ).astype(jnp.int32)
     limits = jnp.concatenate([video_frames, text_len])
 
+    columns = []
+    for values in (in_bias, group_gain, group_bias):
+        rest = values
+        for _ in range(3):
+            term = lax.reduce_precision(rest, 8, 7)
+            columns.append(term.astype(BF16)[:, None])
+            rest = rest - term
     table = jnp.concatenate(
-        [
-            in_weight.reshape(432, 32).T.astype(F32),
-            in_bias[:, None],
-            group_gain[:, None],
-            group_bias[:, None],
-            jnp.zeros((32, 77), F32),
-        ],
-        axis=1,
-    )
-    table = lax.all_gather(table, "chan", axis=0, tiled=True)
-    lane = jnp.arange(512)[None]
-    in_rows = jnp.where(lane < 432, table, 0.0).astype(BF16)
-    columns = table[:, 384:]
+        [in_weight.reshape(432, 32).T] + columns + [jnp.zeros((32, 71), BF16)], axis=1
+    )[None]
+
+    def doubled(held, bit):
+        other = lax.ppermute(held, "chan", [(i, i ^ bit) for i in range(16)])
+        return jnp.concatenate([held, other], axis=0)
 
     packed = pl.pallas_call(
         pack_kernel,
         out_shape=jax.ShapeDtypeStruct((32, 64, HD), BF16),
-        grid_spec=pltpu.PrefetchScalarGridSpec(
-            num_scalar_prefetch=1,
-            grid=(1,),
-            in_specs=[
-                pl.BlockSpec((1152, HD), lambda i, p: (0, 0)),
-                pl.BlockSpec((384, HD), lambda i, p: (p[1], 0)),
-                pl.BlockSpec((1, HD), lambda i, p: (0, 0)),
-                pl.BlockSpec((1, HD), lambda i, p: (0, 0)),
-            ],
-            out_specs=pl.BlockSpec((32, 64, HD), lambda i, p: (0, 0, 0)),
-        ),
+        grid=(1,),
+        in_specs=[
+            pl.BlockSpec((1152, HD), lambda i: (0, 0)),
+            pl.BlockSpec((384, HD), lambda i: (lax.axis_index("frame"), 0)),
+            pl.BlockSpec((1, HD), lambda i: (0, 0)),
+            pl.BlockSpec((1, HD), lambda i: (0, 0)),
+        ],
+        out_specs=pl.BlockSpec((32, 64, HD), lambda i: (0, 0, 0)),
         compiler_params=pltpu.CompilerParams(vmem_limit_bytes=62 * 1024 * 1024),
         name="pack_rows",
     )(
-        place,
         token_qkv.reshape(1152, HD),
         text_kv.reshape(1536, HD),
         query_gain[None],
         key_gain[None],
     )
     rows = lax.all_to_all(packed, ("seq", "frame"), 0, 0, tiled=True)
+    table = doubled(doubled(table, 8), 1)
+    rows, table = lax.optimization_barrier((rows, table))
     attended = pl.pallas_call(
         attend_kernel,
         out_shape=jax.ShapeDtypeStruct((4, 128, HD), BF16),
@@ -304,6 +310,8 @@
         name="project",
     )(attended, out_weight)
     parts = lax.all_to_all(parts, "seq", 0, 0, tiled=True)
+    table = doubled(doubled(table, 4), 2)
+    parts, table = lax.optimization_barrier((parts, table))
     latent = pl.pallas_call(
         latent_kernel,
         out_shape=jax.ShapeDtypeStruct((512, 128), BF16),
@@ -326,21 +334,20 @@
     return pl.pallas_call(
         decode_kernel,
         out_shape=jax.ShapeDtypeStruct((2, 2, 32, 256), BF16),
-        in_specs=[SMEM] + [VMEM] * 5,
+        in_specs=[SMEM] + [VMEM] * 4,
         out_specs=VMEM,
         scratch_shapes=[
             pltpu.VMEM((64, 8, 128), F32),
-            pltpu.VMEM((59, 16, 256), F32),
+            pltpu.VMEM((16, 32, DCH), F32),
+            pltpu.VMEM((54, 16, 256), F32),
             pltpu.VMEM((2, 16, 32, 256), F32),
-            pltpu.VMEM((4, DCH, 256), F32),
         ],
         compiler_params=PARAMS,
         name="decode",
     )(
         place,
         latent.reshape(512, 128),
-        in_rows,
-        columns,
+        table,
         conv_weight.transpose(0, 2, 1),
         conv_bias[:, None],
     )

time: 127 us -> 113 us (0.89)
  waiting for transfers between devices: 52.5 us -> 32 us
  blocking collectives: 10 us -> 27.7 us
  between operations: 14.9 us -> 1.5 us
  starting transfers between devices: 31 us -> 36.4 us
  other arithmetic: 2.11 us -> 0.28 us
  Pallas kernels: 13.5 us -> 12.1 us
    all_to_all x0 -> x1, blocking collectives: none -> 18 us  [on_device(): lax.all_to_all(latent.reshape(64, 8, 128), ('chan', 'frame'), 0, 0, tiled...]
    all_to_all x1, waiting for transfers between devices: 21 us -> 5.03 us  [on_device(): parts = lax.all_to_all(parts, 'seq', 0, 0, tiled=True)]
    ppermute x0 -> x4, waiting for transfers between devices: none -> 15.3 us  [doubled(): other = lax.ppermute(held, 'chan', [(i, i ^ bit) for i in range(16)])]
    ppermute x0 -> x4, starting transfers between devices: none -> 13.5 us  [doubled(): other = lax.ppermute(held, 'chan', [(i, i ^ bit) for i in range(16)])]
    all_to_all x1, waiting for transfers between devices: 14.6 us -> 2.8 us  [on_device(): rows = lax.all_to_all(packed, ('seq', 'frame'), 0, 0, tiled=True)]
    all_to_all x1 -> x0, starting transfers between devices: 10 us -> none  [on_device(): lax.all_to_all(latent.reshape(64, 8, 128), ('chan', 'frame'), 0, 0, tiled...]
    all_to_all x1 -> x0, waiting for transfers between devices: 9.25 us -> none  [on_device(): lax.all_to_all(latent.reshape(64, 8, 128), ('chan', 'frame'), 0, 0, tiled...]
    all_to_all x1, starting transfers between devices: 3.68 us -> 5.72 us  [on_device(): parts = lax.all_to_all(parts, 'seq', 0, 0, tiled=True)]
  transfers between devices with their start and end apart: 5 -> 7, of which waited for: 4 -> 7; matrix products, arithmetic and copies ran while one was open for 3% -> 2% of each run, Pallas kernels for 4% -> 0%
where the time goes in v2:
time: 113 us; the launch traced here: 112 us
  starting transfers between devices  36.4 us (32%)
  waiting for transfers between devices  32 us (28%)
  blocking collectives  27.7 us (25%)
  Pallas kernels  12.1 us (11%)
  local copies, waits for them, and re-layouts  2.23 us (2%)
  between operations  1.5 us (1%)
    all_to_all x1, blocking collectives, on_device(): lax.all_to_all(latent.reshape(64, 8, 128), ('chan', 'frame'), 0, 0, tiled...  18 us
    ppermute x4, waiting for transfers between devices, doubled(): other = lax.ppermute(held, 'chan', [(i, i ^ bit) for i in range(16)])  15.3 us
    all_to_all x1, starting transfers between devices, on_device(): rows = lax.all_to_all(packed, ('seq', 'frame'), 0, 0, tiled=True)  13.9 us
    ppermute x4, starting transfers between devices, doubled(): other = lax.ppermute(held, 'chan', [(i, i ^ bit) for i in range(16)])  13.5 us
    all_to_all x1, blocking collectives, on_device(): attended = lax.all_to_all(attended, 'frame', 0, 0, tiled=True)  9.72 us
    all_to_all x1, waiting for transfers between devices, on_device(): latent = lax.all_to_all(latent, 'seq', 0, 0, tiled=True)  8.9 us
    all_to_all x1, starting transfers between devices, on_device(): parts = lax.all_to_all(parts, 'seq', 0, 0, tiled=True)  5.72 us
    pallas_call x1, Pallas kernels, on_device(): pl.pallas_call(decode_kernel, out_shape=jax.ShapeDtypeStruct((2, 2, 32, 2...  5.21 us
  transfers between devices with their start and end apart: 7, of which 7 were waited for; matrix products, arithmetic and copies ran while one was open for 2% of the time, Pallas kernels for 0%

profile of v2, /device:TPU:2, one launch (start us, length us, event | category | flops | bytes accessed | tf_op | source)
XLA Modules:
  0.0 112.2 jit_solution(9246745271637161984)
XLA Ops:
  0.0 2.1 %pack_rows.1 = bf16[32,64,128]{2,1,0:T(8,128)(2,1)} custom-call(bf16[1152,128]{1,0:T(8,128)(2,1)} %bitcast.41, bf16[1536,128]{1,0:T(8,128)(2,1)} %bitcast.40, f32[1,128]{1,0:T(1,128)} %bitcast.47, f32[1,128]{1,0:T(1,128)} %bitcast.48), custom_call_target="tpu_custom_call" | custom-call | tf_op jit(solution)/shard_map/pack_rows/pallas_call | solution.py:273
  2.1 13.9 %all-to-all-start = ((bf16[32,64,128]{2,1,0:T(8,128)(2,1)}), bf16[32,64,128]{2,1,0:T(8,128)(2,1)S(1)}, u32[]{:S(2)}, u32[]{:S(2)}) async-start(bf16[32,64,128]{2,1,0:T(8,128)(2,1)} %pack_rows.1), calls=%async_computation | async-start | bytes 1048576 | tf_op jit(solution)/shard_map/all_to_all | solution.py:292
  16.0 1.0 copy.32
  17.0 0.0 copy-done.9
  17.0 0.1 copy.33
  17.1 0.1 copy.34
  17.2 0.1 copy.35
  17.3 0.0 copy-done.10
  17.4 0.1 copy.36
  17.5 0.1 copy.37
  17.6 0.1 copy.38
  17.7 0.0 copy-done.11
  17.7 0.1 copy.39
  17.8 0.1 copy.40
  17.9 0.1 copy.41
  18.0 0.1 concatenate.21
  18.1 5.0 %collective-permute-start = (bf16[1,32,512]{2,1,0:T(8,128)(2,1)S(1)}, bf16[1,32,512]{2,1,0:T(8,128)(2,1)S(1)}, u32[]{:S(2)}, u32[]{:S(2)}) collective-permute-start(bf16[1,32,512]{2,1,0:T(8,128)(2,1)S(1)} %bitcast.42), channel_id=1, source_target_pairs={{0,32},{4,36},{8,40},{12,44},{16,48},{20,52},{24,56},{28,60},{32,0... | collective-permute-start | bytes 98312 | tf_op jit(solution)/shard_map/ppermute | solution.py:270
  24.4 4.2 %collective-permute-done = bf16[1,32,512]{2,1,0:T(8,128)(2,1)S(1)} collective-permute-done((bf16[1,32,512]{2,1,0:T(8,128)(2,1)S(1)}, bf16[1,32,512]{2,1,0:T(8,128)(2,1)S(1)}, u32[]{:S(2)}, u32[]{:S(2)}) %collective-permute-start) | collective-permute-done | bytes 32800 | tf_op jit(solution)/shard_map/ppermute | solution.py:270
  28.7 1.9 %collective-permute-start.1 = (bf16[2,32,512]{2,1,0:T(8,128)(2,1)S(1)}, bf16[2,32,512]{2,1,0:T(8,128)(2,1)S(1)}, u32[]{:S(2)}, u32[]{:S(2)}) collective-permute-start(bf16[2,32,512]{2,1,0:T(8,128)(2,1)S(1)} %pad_maximum_fusion.3), channel_id=1, source_target_pairs={{0,4},{4,0},{8,12},{12,8},{16,20},{20,16},{24,28},{28,24},{32,36},... | collective-permute-start | bytes 196616 | tf_op jit(solution)/shard_map/ppermute | solution.py:270
  30.6 0.1 pad_add_fusion.1.limits
  30.7 1.1 %collective-permute-done.1 = bf16[2,32,512]{2,1,0:T(8,128)(2,1)S(1)} collective-permute-done((bf16[2,32,512]{2,1,0:T(8,128)(2,1)S(1)}, bf16[2,32,512]{2,1,0:T(8,128)(2,1)S(1)}, u32[]{:S(2)}, u32[]{:S(2)}) %collective-permute-start.1) | collective-permute-done | bytes 65568 | tf_op jit(solution)/shard_map/ppermute | solution.py:270
  31.8 2.8 %all-to-all-done = bf16[32,64,128]{2,1,0:T(8,128)(2,1)S(1)} async-done(((bf16[32,64,128]{2,1,0:T(8,128)(2,1)}), bf16[32,64,128]{2,1,0:T(8,128)(2,1)S(1)}, u32[]{:S(2)}, u32[]{:S(2)}) %all-to-all-start) | async-done | bytes 524320 | tf_op jit(solution)/shard_map/all_to_all | solution.py:292
  34.6 2.0 %attend.1 = bf16[4,128,128]{2,1,0:T(8,128)(2,1)S(1)} custom-call(s32[2]{0:T(128)S(1)} %pad_add_fusion.1.limits, bf16[8,4,64,128]{3,2,1,0:T(8,128)(2,1)S(1)} %bitcast.35), custom_call_target="tpu_custom_call" | custom-call | tf_op jit(solution)/shard_map/attend/pallas_call | solution.py:295
  36.6 9.7 %all_to_all.25.attended_ref = bf16[4,128,128]{2,1,0:T(8,128)(2,1)S(1)} all-to-all(bf16[4,128,128]{2,1,0:T(8,128)(2,1)S(1)} %attend.1), channel_id=1, replica_groups=mesh['seq'=8,'chan'=16,'frame'=4] {'frame'}, dimensions={0} | all-to-all | bytes 262144 | tf_op jit(solution)/shard_map/all_to_all | solution.py:303
  46.3 0.0 copy-done
  46.3 1.5 %project.1 = bf16[8,16,3072]{2,1,0:T(8,128)(2,1)} custom-call(bf16[4,128,128]{2,1,0:T(8,128)(2,1)S(1)} %all_to_all.25.attended_ref, bf16[3,128,3072]{2,1,0:T(8,128)(2,1)S(1)} %copy-done), custom_call_target="tpu_custom_call" | custom-call | tf_op jit(solution)/shard_map/project/pallas_call | solution.py:304
  47.8 0.0 copy-start.6
  47.8 0.0 copy-start.8
  47.8 0.0 copy-start.1
  47.8 5.7 %all-to-all-start.2 = ((bf16[8,16,3072]{2,1,0:T(8,128)(2,1)}), bf16[8,16,3072]{2,1,0:T(8,128)(2,1)S(1)}, u32[]{:S(2)}, u32[]{:S(2)}) async-start(bf16[8,16,3072]{2,1,0:T(8,128)(2,1)} %project.1), calls=%async_computation.2 | async-start | bytes 1572864 | tf_op jit(solution)/shard_map/all_to_all | solution.py:312
  53.6 4.0 %collective-permute-start.2 = (bf16[4,32,512]{2,1,0:T(8,128)(2,1)S(1)}, bf16[4,32,512]{2,1,0:T(8,128)(2,1)S(1)}, u32[]{:S(2)}, u32[]{:S(2)}) collective-permute-start(bf16[4,32,512]{2,1,0:T(8,128)(2,1)S(1)} %pad_maximum_fusion.2), channel_id=1, source_target_pairs={{0,16},{4,20},{8,24},{12,28},{16,0},{20,4},{24,8},{28,12},{32,48},... | collective-permute-start | bytes 393224 | tf_op jit(solution)/shard_map/ppermute | solution.py:270
  57.6 4.3 %collective-permute-done.2 = bf16[4,32,512]{2,1,0:T(8,128)(2,1)S(1)} collective-permute-done((bf16[4,32,512]{2,1,0:T(8,128)(2,1)S(1)}, bf16[4,32,512]{2,1,0:T(8,128)(2,1)S(1)}, u32[]{:S(2)}, u32[]{:S(2)}) %collective-permute-start.2) | collective-permute-done | bytes 131104 | tf_op jit(solution)/shard_map/ppermute | solution.py:270
  61.9 2.5 %collective-permute-start.3 = (bf16[8,32,512]{2,1,0:T(8,128)(2,1)S(1)}, bf16[8,32,512]{2,1,0:T(8,128)(2,1)S(1)}, u32[]{:S(2)}, u32[]{:S(2)}) collective-permute-start(bf16[8,32,512]{2,1,0:T(8,128)(2,1)S(1)} %pad_maximum_fusion.1), channel_id=1, source_target_pairs={{0,8},{4,12},{8,0},{12,4},{16,24},{20,28},{24,16},{28,20},{32,40},... | collective-permute-start | bytes 786440 | tf_op jit(solution)/shard_map/ppermute | solution.py:270
  64.4 0.0 copy-done.7
  64.4 0.1 copy.42.bias_ref
  64.5 0.1 pad_add_fusion.place
  64.6 5.6 %collective-permute-done.3 = bf16[8,32,512]{2,1,0:T(8,128)(2,1)S(1)} collective-permute-done((bf16[8,32,512]{2,1,0:T(8,128)(2,1)S(1)}, bf16[8,32,512]{2,1,0:T(8,128)(2,1)S(1)}, u32[]{:S(2)}, u32[]{:S(2)}) %collective-permute-start.3) | collective-permute-done | bytes 262176 | tf_op jit(solution)/shard_map/ppermute | solution.py:270
  70.2 0.1 pad_maximum_fusion.table_ref
  70.3 5.0 %all-to-all-done.2.parts_ref = bf16[8,16,3072]{2,1,0:T(8,128)(2,1)S(1)} async-done(((bf16[8,16,3072]{2,1,0:T(8,128)(2,1)}), bf16[8,16,3072]{2,1,0:T(8,128)(2,1)S(1)}, u32[]{:S(2)}, u32[]{:S(2)}) %all-to-all-start.2) | async-done | bytes 786464 | tf_op jit(solution)/shard_map/all_to_all | solution.py:312
  75.3 0.0 copy-done.2
  75.3 0.0 copy-done.3
  75.3 0.0 copy-done.4
  75.3 1.3 %latents.1 = bf16[512,128]{1,0:T(8,128)(2,1)S(1)} custom-call(s32[3]{0:T(128)S(1)} %pad_add_fusion.place, bf16[8,16,3072]{2,1,0:T(8,128)(2,1)S(1)} %all-to-all-done.2.parts_ref, bf16[16,3072]{1,0:T(8,128)(2,1)S(1)} %bitcast.39, f32[1,3072]{1,0:T(1,128)S(1)} %copy-done.4, f32[1,3072]{1,0:T(1,128)S(1)} %copy-done.5, f32[1,3072]{1,0:T(1,128)S(1)} %copy-done.6, ...), custom_call_target="tpu_custom_call" | custom-call | tf_op jit(solution)/shard_map/latents/pallas_call | solution.py:315
  76.7 18.0 %all_to_all.26 = bf16[64,8,128]{2,1,0:T(8,128)(2,1)} all-to-all(bf16[64,8,128]{2,1,0:T(8,128)(2,1)S(1)} %bitcast.38), channel_id=1, replica_groups=mesh['seq'=8,'chan'=16,'frame'=4] {'chan','frame'}, dimensions={0} | all-to-all | bytes 262144 | tf_op jit(solution)/shard_map/all_to_all | solution.py:332
  94.6 3.4 %all-to-all-start.4 = ((bf16[64,8,128]{2,1,0:T(8,128)(2,1)}), bf16[64,8,128]{2,1,0:T(8,128)(2,1)S(1)}, u32[]{:S(2)}, u32[]{:S(2)}) async-start(bf16[64,8,128]{2,1,0:T(8,128)(2,1)} %all_to_all.26), calls=%async_computation.4 | async-start | bytes 262144 | tf_op jit(solution)/shard_map/all_to_all | solution.py:333
  98.0 0.1 copy.43.bias_ref
  98.1 8.9 %all-to-all-done.4 = bf16[64,8,128]{2,1,0:T(8,128)(2,1)S(1)} async-done(((bf16[64,8,128]{2,1,0:T(8,128)(2,1)}), bf16[64,8,128]{2,1,0:T(8,128)(2,1)S(1)}, u32[]{:S(2)}, u32[]{:S(2)}) %all-to-all-start.4) | async-done | bytes 131104 | tf_op jit(solution)/shard_map/all_to_all | solution.py:333
  107.0 5.2 %decode.1 = bf16[2,2,32,256]{3,2,1,0:T(8,128)(2,1)} custom-call(s32[3]{0:T(128)S(1)} %pad_add_fusion.place, bf16[512,128]{1,0:T(8,128)(2,1)S(1)} %bitcast.37, bf16[16,32,512]{2,1,0:T(8,128)(2,1)S(1)} %pad_maximum_fusion.table_ref, bf16[27,32,512]{2,1,0:T(8,128)(2,1)S(1)} %bitcast.36, f32[32,1]{1,0:T(8,128)S(1)} %copy.43.bias_ref), custom_call_target="tpu_custom_call" | custom-call | tf_op jit(solution)/shard_map/decode/pallas_call | solution.py:334
  (20 shorter events, 0.1 us)
Async XLA Ops:
  0.0 17.0 %copy-start.9 = (f32[32]{0:T(128)S(1)}, f32[32]{0:T(128)}, u32[]{:S(2)}) copy-start(f32[32]{0:T(128)} %param.33) | copy-start | bytes 388
  0.0 17.3 %copy-start.10 = (f32[32]{0:T(128)S(1)}, f32[32]{0:T(128)}, u32[]{:S(2)}) copy-start(f32[32]{0:T(128)} %param.34) | copy-start | bytes 388
  0.0 17.6 %copy-start.11 = (f32[32]{0:T(128)S(1)}, f32[32]{0:T(128)}, u32[]{:S(2)}) copy-start(f32[32]{0:T(128)} %param.35) | copy-start | bytes 388
  2.1 44.2 %copy-start = (bf16[3,128,3072]{2,1,0:T(8,128)(2,1)S(1)}, bf16[3,128,3072]{2,1,0:T(8,128)(2,1)}, u32[]{:S(2)}) copy-start(bf16[3,128,3072]{2,1,0:T(8,128)(2,1)} %weight_ref.2) | copy-start | bytes 7077892
  2.1 32.5 %all-to-all-start = ((bf16[32,64,128]{2,1,0:T(8,128)(2,1)}), bf16[32,64,128]{2,1,0:T(8,128)(2,1)S(1)}, u32[]{:S(2)}, u32[]{:S(2)}) async-start(bf16[32,64,128]{2,1,0:T(8,128)(2,1)} %pack_rows.1), calls=%async_computation | async-start | bytes 1048576 | tf_op jit(solution)/shard_map/all_to_all | solution.py:292
  18.1 10.6 %collective-permute-start = (bf16[1,32,512]{2,1,0:T(8,128)(2,1)S(1)}, bf16[1,32,512]{2,1,0:T(8,128)(2,1)S(1)}, u32[]{:S(2)}, u32[]{:S(2)}) collective-permute-start(bf16[1,32,512]{2,1,0:T(8,128)(2,1)S(1)} %bitcast.42), channel_id=1, source_target_pairs={{0,32},{4,36},{8,40},{12,44},{16,48},{20,52},{24,56},{28,60},{32,0... | collective-permute-start | bytes 98312 | tf_op jit(solution)/shard_map/ppermute | solution.py:270
  28.7 3.1 %collective-permute-start.1 = (bf16[2,32,512]{2,1,0:T(8,128)(2,1)S(1)}, bf16[2,32,512]{2,1,0:T(8,128)(2,1)S(1)}, u32[]{:S(2)}, u32[]{:S(2)}) collective-permute-start(bf16[2,32,512]{2,1,0:T(8,128)(2,1)S(1)} %pad_maximum_fusion.3), channel_id=1, source_target_pairs={{0,4},{4,0},{8,12},{12,8},{16,20},{20,16},{24,28},{28,24},{32,36},... | collective-permute-start | bytes 196616 | tf_op jit(solution)/shard_map/ppermute | solution.py:270
  46.3 18.1 %copy-start.7 = (f32[64]{0:T(128)S(1)}, f32[64]{0:T(128)}, u32[]{:S(2)}) copy-start(f32[64]{0:T(128)} %param.29) | copy-start | bytes 772
  47.8 27.5 %copy-start.2 = (bf16[64,3072]{1,0:T(8,128)(2,1)S(1)}, bf16[64,3072]{1,0:T(8,128)(2,1)}, u32[]{:S(2)}) copy-start(bf16[64,3072]{1,0:T(8,128)(2,1)} %weight_ref.3) | copy-start | bytes 1179652
  47.8 27.5 %copy-start.3 = (bf16[1,2,8,3072]{3,2,1,0:T(8,128)(2,1)S(1)}, bf16[1,2,8,3072]{3,2,1,0:T(8,128)(2,1)}, u32[]{:S(2)}) copy-start(bf16[1,2,8,3072]{3,2,1,0:T(8,128)(2,1)} %param.21) | copy-start | bytes 294916
  47.8 27.5 %copy-start.4 = (f32[1,3072]{1,0:T(1,128)S(1)}, f32[1,3072]{1,0:T(1,128)}, u32[]{:S(2)}) copy-start(f32[1,3072]{1,0:T(1,128)} %gate_ref.1) | copy-start | bytes 36868
  47.8 27.5 %copy-start.5 = (f32[1,3072]{1,0:T(1,128)S(1)}, f32[1,3072]{1,0:T(1,128)}, u32[]{:S(2)}) copy-start(f32[1,3072]{1,0:T(1,128)} %shift_ref.1) | copy-start | bytes 36868
  47.8 27.5 %copy-start.6 = (f32[1,3072]{1,0:T(1,128)S(1)}, f32[1,3072]{1,0:T(1,128)}, u32[]{:S(2)}) copy-start(f32[1,3072]{1,0:T(1,128)} %scale_ref.1) | copy-start | bytes 36868
  47.8 50.2 %copy-start.8 = (f32[32]{0:T(128)S(1)}, f32[32]{0:T(128)}, u32[]{:S(2)}) copy-start(f32[32]{0:T(128)} %param.37) | copy-start | bytes 388
  47.8 59.2 %copy-start.1 = (bf16[27,512,32]{1,2,0:T(8,128)(2,1)S(1)}, bf16[27,512,32]{1,2,0:T(8,128)(2,1)}, u32[]{:S(2)}) copy-start(bf16[27,512,32]{1,2,0:T(8,128)(2,1)} %param.36) | copy-start | bytes 2654212
  47.8 27.5 %all-to-all-start.2 = ((bf16[8,16,3072]{2,1,0:T(8,128)(2,1)}), bf16[8,16,3072]{2,1,0:T(8,128)(2,1)S(1)}, u32[]{:S(2)}, u32[]{:S(2)}) async-start(bf16[8,16,3072]{2,1,0:T(8,128)(2,1)} %project.1), calls=%async_computation.2 | async-start | bytes 1572864 | tf_op jit(solution)/shard_map/all_to_all | solution.py:312
  53.6 8.4 %collective-permute-start.2 = (bf16[4,32,512]{2,1,0:T(8,128)(2,1)S(1)}, bf16[4,32,512]{2,1,0:T(8,128)(2,1)S(1)}, u32[]{:S(2)}, u32[]{:S(2)}) collective-permute-start(bf16[4,32,512]{2,1,0:T(8,128)(2,1)S(1)} %pad_maximum_fusion.2), channel_id=1, source_target_pairs={{0,16},{4,20},{8,24},{12,28},{16,0},{20,4},{24,8},{28,12},{32,48},... | collective-permute-start | bytes 393224 | tf_op jit(solution)/shard_map/ppermute | solution.py:270
  61.9 8.3 %collective-permute-start.3 = (bf16[8,32,512]{2,1,0:T(8,128)(2,1)S(1)}, bf16[8,32,512]{2,1,0:T(8,128)(2,1)S(1)}, u32[]{:S(2)}, u32[]{:S(2)}) collective-permute-start(bf16[8,32,512]{2,1,0:T(8,128)(2,1)S(1)} %pad_maximum_fusion.1), channel_id=1, source_target_pairs={{0,8},{4,12},{8,0},{12,4},{16,24},{20,28},{24,16},{28,20},{32,40},... | collective-permute-start | bytes 786440 | tf_op jit(solution)/shard_map/ppermute | solution.py:270
  94.6 12.4 %all-to-all-start.4 = ((bf16[64,8,128]{2,1,0:T(8,128)(2,1)}), bf16[64,8,128]{2,1,0:T(8,128)(2,1)S(1)}, u32[]{:S(2)}, u32[]{:S(2)}) async-start(bf16[64,8,128]{2,1,0:T(8,128)(2,1)} %all_to_all.26), calls=%async_computation.4 | async-start | bytes 262144 | tf_op jit(solution)/shard_map/all_to_all | solution.py:333

commit v3 on v2

--- a/solution.py
+++ b/solution.py
@@ -149,7 +149,7 @@
     chan = place[0]
     frame = place[1]
     def position(v):
-        return ((v >> 3) & 1) | ((v & 1) << 1) | (v & 4) | ((v & 2) << 2)
+        return ((v >> 3) & 1) | ((v & 4) >> 1) | ((v & 2) << 1) | ((v & 1) << 3)
 
     table_scratch[...] = table_ref[...].astype(F32)
     table = jnp.concatenate(
@@ -290,7 +290,7 @@
         key_gain[None],
     )
     rows = lax.all_to_all(packed, ("seq", "frame"), 0, 0, tiled=True)
-    table = doubled(doubled(table, 8), 1)
+    table = doubled(table, 8)
     rows, table = lax.optimization_barrier((rows, table))
     attended = pl.pallas_call(
         attend_kernel,
@@ -310,7 +310,7 @@
         name="project",
     )(attended, out_weight)
     parts = lax.all_to_all(parts, "seq", 0, 0, tiled=True)
-    table = doubled(doubled(table, 4), 2)
+    table = doubled(doubled(doubled(table, 4), 2), 1)
     parts, table = lax.optimization_barrier((parts, table))
     latent = pl.pallas_call(
         latent_kernel,

time: 113 us -> 111 us (0.982)
  waiting for transfers between devices: 32 us -> 30.8 us
    all_to_all x1, waiting for transfers between devices: 2.8 us -> 5.97 us  [on_device(): rows = lax.all_to_all(packed, ('seq', 'frame'), 0, 0, tiled=True)]
    all_to_all x1, waiting for transfers between devices: 5.03 us -> 2.43 us  [on_device(): parts = lax.all_to_all(parts, 'seq', 0, 0, tiled=True)]
    all_to_all x1, starting transfers between devices: 5.72 us -> 3.69 us  [on_device(): parts = lax.all_to_all(parts, 'seq', 0, 0, tiled=True)]
    ppermute x4, waiting for transfers between devices: 15.3 us -> 13.5 us  [doubled(): other = lax.ppermute(held, 'chan', [(i, i ^ bit) for i in range(16)])]
    all_to_all x1, starting transfers between devices: 3.37 us -> 4.76 us  [on_device(): latent = lax.all_to_all(latent, 'seq', 0, 0, tiled=True)]
where the time goes in v3:
time: 111 us
  starting transfers between devices  35.8 us (32%)
  waiting for transfers between devices  30.8 us (28%)
  blocking collectives  28 us (25%)
  Pallas kernels  12.1 us (11%)
  local copies, waits for them, and re-layouts  2.23 us (2%)
  between operations  1.49 us (1%)
    all_to_all x1, blocking collectives, on_device(): lax.all_to_all(latent.reshape(64, 8, 128), ('chan', 'frame'), 0, 0, tiled...  18.3 us
    all_to_all x1, starting transfers between devices, on_device(): rows = lax.all_to_all(packed, ('seq', 'frame'), 0, 0, tiled=True)  13.9 us
    ppermute x4, starting transfers between devices, doubled(): other = lax.ppermute(held, 'chan', [(i, i ^ bit) for i in range(16)])  13.5 us
    ppermute x4, waiting for transfers between devices, doubled(): other = lax.ppermute(held, 'chan', [(i, i ^ bit) for i in range(16)])  13.5 us
    all_to_all x1, blocking collectives, on_device(): attended = lax.all_to_all(attended, 'frame', 0, 0, tiled=True)  9.72 us
    all_to_all x1, waiting for transfers between devices, on_device(): latent = lax.all_to_all(latent, 'seq', 0, 0, tiled=True)  8.98 us
    all_to_all x1, waiting for transfers between devices, on_device(): rows = lax.all_to_all(packed, ('seq', 'frame'), 0, 0, tiled=True)  5.97 us
    pallas_call x1, Pallas kernels, on_device(): pl.pallas_call(decode_kernel, out_shape=jax.ShapeDtypeStruct((2, 2, 32, 2...  5.21 us
  transfers between devices with their start and end apart: 7, of which 7 were waited for; matrix products, arithmetic and copies ran while one was open for 2% of the time, Pallas kernels for 0%

profile of v3, /device:TPU:2, one launch (start us, length us, event | category | flops | bytes accessed | tf_op | source)
XLA Modules:
  0.0 110.7 jit_solution(804491962641880206)
XLA Ops:
  0.0 2.1 %pack_rows.1 = bf16[32,64,128]{2,1,0:T(8,128)(2,1)} custom-call(bf16[1152,128]{1,0:T(8,128)(2,1)} %bitcast.41, bf16[1536,128]{1,0:T(8,128)(2,1)} %bitcast.40, f32[1,128]{1,0:T(1,128)} %bitcast.46, f32[1,128]{1,0:T(1,128)} %bitcast.47), custom_call_target="tpu_custom_call" | custom-call | tf_op jit(solution)/shard_map/pack_rows/pallas_call | solution.py:273
  2.1 13.9 %all-to-all-start = ((bf16[32,64,128]{2,1,0:T(8,128)(2,1)}), bf16[32,64,128]{2,1,0:T(8,128)(2,1)S(1)}, u32[]{:S(2)}, u32[]{:S(2)}) async-start(bf16[32,64,128]{2,1,0:T(8,128)(2,1)} %pack_rows.1), calls=%async_computation | async-start | bytes 1048576 | tf_op jit(solution)/shard_map/all_to_all | solution.py:292
  16.0 1.0 copy.32
  17.0 0.0 copy-done.9
  17.0 0.1 copy.33
  17.1 0.1 copy.34
  17.2 0.1 copy.35
  17.3 0.0 copy-done.10
  17.4 0.1 copy.36
  17.5 0.1 copy.37
  17.6 0.1 copy.38
  17.7 0.0 copy-done.11
  17.7 0.1 copy.39
  17.8 0.1 copy.40
  17.9 0.1 copy.41
  18.0 0.1 concatenate.21
  18.1 5.0 %collective-permute-start = (bf16[1,32,512]{2,1,0:T(8,128)(2,1)S(1)}, bf16[1,32,512]{2,1,0:T(8,128)(2,1)S(1)}, u32[]{:S(2)}, u32[]{:S(2)}) collective-permute-start(bf16[1,32,512]{2,1,0:T(8,128)(2,1)S(1)} %bitcast.43), channel_id=1, source_target_pairs={{0,32},{4,36},{8,40},{12,44},{16,48},{20,52},{24,56},{28,60},{32,0... | collective-permute-start | bytes 98312 | tf_op jit(solution)/shard_map/ppermute | solution.py:270
  24.4 0.1 pad_add_fusion.1.limits
  24.5 4.2 %collective-permute-done = bf16[1,32,512]{2,1,0:T(8,128)(2,1)S(1)} collective-permute-done((bf16[1,32,512]{2,1,0:T(8,128)(2,1)S(1)}, bf16[1,32,512]{2,1,0:T(8,128)(2,1)S(1)}, u32[]{:S(2)}, u32[]{:S(2)}) %collective-permute-start) | collective-permute-done | bytes 32800 | tf_op jit(solution)/shard_map/ppermute | solution.py:270
  28.7 6.0 %all-to-all-done = bf16[32,64,128]{2,1,0:T(8,128)(2,1)S(1)} async-done(((bf16[32,64,128]{2,1,0:T(8,128)(2,1)}), bf16[32,64,128]{2,1,0:T(8,128)(2,1)S(1)}, u32[]{:S(2)}, u32[]{:S(2)}) %all-to-all-start) | async-done | bytes 524320 | tf_op jit(solution)/shard_map/all_to_all | solution.py:292
  34.6 2.0 %attend.1 = bf16[4,128,128]{2,1,0:T(8,128)(2,1)S(1)} custom-call(s32[2]{0:T(128)S(1)} %pad_add_fusion.1.limits, bf16[8,4,64,128]{3,2,1,0:T(8,128)(2,1)S(1)} %bitcast.35), custom_call_target="tpu_custom_call" | custom-call | tf_op jit(solution)/shard_map/attend/pallas_call | solution.py:295
  36.6 9.7 %all_to_all.25.attended_ref = bf16[4,128,128]{2,1,0:T(8,128)(2,1)S(1)} all-to-all(bf16[4,128,128]{2,1,0:T(8,128)(2,1)S(1)} %attend.1), channel_id=1, replica_groups=mesh['seq'=8,'chan'=16,'frame'=4] {'frame'}, dimensions={0} | all-to-all | bytes 262144 | tf_op jit(solution)/shard_map/all_to_all | solution.py:303
  46.3 0.0 copy-done
  46.3 1.5 %project.1 = bf16[8,16,3072]{2,1,0:T(8,128)(2,1)} custom-call(bf16[4,128,128]{2,1,0:T(8,128)(2,1)S(1)} %all_to_all.25.attended_ref, bf16[3,128,3072]{2,1,0:T(8,128)(2,1)S(1)} %copy-done), custom_call_target="tpu_custom_call" | custom-call | tf_op jit(solution)/shard_map/project/pallas_call | solution.py:304
  47.8 0.0 copy-start.6
  47.8 0.0 copy-start.8
  47.8 0.0 copy-start.1
  47.8 3.7 %all-to-all-start.2 = ((bf16[8,16,3072]{2,1,0:T(8,128)(2,1)}), bf16[8,16,3072]{2,1,0:T(8,128)(2,1)S(1)}, u32[]{:S(2)}, u32[]{:S(2)}) async-start(bf16[8,16,3072]{2,1,0:T(8,128)(2,1)} %project.1), calls=%async_computation.2 | async-start | bytes 1572864 | tf_op jit(solution)/shard_map/all_to_all | solution.py:312
  51.5 4.1 %collective-permute-start.1 = (bf16[2,32,512]{2,1,0:T(8,128)(2,1)S(1)}, bf16[2,32,512]{2,1,0:T(8,128)(2,1)S(1)}, u32[]{:S(2)}, u32[]{:S(2)}) collective-permute-start(bf16[2,32,512]{2,1,0:T(8,128)(2,1)S(1)} %pad_maximum_fusion.3), channel_id=1, source_target_pairs={{0,16},{4,20},{8,24},{12,28},{16,0},{20,4},{24,8},{28,12},{32,48},... | collective-permute-start | bytes 196616 | tf_op jit(solution)/shard_map/ppermute | solution.py:270
  55.6 3.6 %collective-permute-done.1 = bf16[2,32,512]{2,1,0:T(8,128)(2,1)S(1)} collective-permute-done((bf16[2,32,512]{2,1,0:T(8,128)(2,1)S(1)}, bf16[2,32,512]{2,1,0:T(8,128)(2,1)S(1)}, u32[]{:S(2)}, u32[]{:S(2)}) %collective-permute-start.1) | collective-permute-done | bytes 65568 | tf_op jit(solution)/shard_map/ppermute | solution.py:270
  59.2 2.4 %collective-permute-start.2 = (bf16[4,32,512]{2,1,0:T(8,128)(2,1)S(1)}, bf16[4,32,512]{2,1,0:T(8,128)(2,1)S(1)}, u32[]{:S(2)}, u32[]{:S(2)}) collective-permute-start(bf16[4,32,512]{2,1,0:T(8,128)(2,1)S(1)} %pad_maximum_fusion.2), channel_id=1, source_target_pairs={{0,8},{4,12},{8,0},{12,4},{16,24},{20,28},{24,16},{28,20},{32,40},... | collective-permute-start | bytes 393224 | tf_op jit(solution)/shard_map/ppermute | solution.py:270
  61.7 4.4 %collective-permute-done.2 = bf16[4,32,512]{2,1,0:T(8,128)(2,1)S(1)} collective-permute-done((bf16[4,32,512]{2,1,0:T(8,128)(2,1)S(1)}, bf16[4,32,512]{2,1,0:T(8,128)(2,1)S(1)}, u32[]{:S(2)}, u32[]{:S(2)}) %collective-permute-start.2) | collective-permute-done | bytes 131104 | tf_op jit(solution)/shard_map/ppermute | solution.py:270
  66.1 1.9 %collective-permute-start.3 = (bf16[8,32,512]{2,1,0:T(8,128)(2,1)S(1)}, bf16[8,32,512]{2,1,0:T(8,128)(2,1)S(1)}, u32[]{:S(2)}, u32[]{:S(2)}) collective-permute-start(bf16[8,32,512]{2,1,0:T(8,128)(2,1)S(1)} %pad_maximum_fusion.1), channel_id=1, source_target_pairs={{0,4},{4,0},{8,12},{12,8},{16,20},{20,16},{24,28},{28,24},{32,36},... | collective-permute-start | bytes 786440 | tf_op jit(solution)/shard_map/ppermute | solution.py:270
  68.0 0.0 copy-done.7
  68.1 0.1 copy.42.bias_ref
  68.1 0.1 pad_add_fusion.place
  68.2 1.3 %collective-permute-done.3 = bf16[8,32,512]{2,1,0:T(8,128)(2,1)S(1)} collective-permute-done((bf16[8,32,512]{2,1,0:T(8,128)(2,1)S(1)}, bf16[8,32,512]{2,1,0:T(8,128)(2,1)S(1)}, u32[]{:S(2)}, u32[]{:S(2)}) %collective-permute-start.3) | collective-permute-done | bytes 262176 | tf_op jit(solution)/shard_map/ppermute | solution.py:270
  69.5 0.1 pad_maximum_fusion.table_ref
  69.6 2.4 %all-to-all-done.2.parts_ref = bf16[8,16,3072]{2,1,0:T(8,128)(2,1)S(1)} async-done(((bf16[8,16,3072]{2,1,0:T(8,128)(2,1)}), bf16[8,16,3072]{2,1,0:T(8,128)(2,1)S(1)}, u32[]{:S(2)}, u32[]{:S(2)}) %all-to-all-start.2) | async-done | bytes 786464 | tf_op jit(solution)/shard_map/all_to_all | solution.py:312
  72.0 0.0 copy-done.2
  72.0 0.0 copy-done.3
  72.0 0.0 copy-done.4
  72.1 1.3 %latents.1 = bf16[512,128]{1,0:T(8,128)(2,1)S(1)} custom-call(s32[3]{0:T(128)S(1)} %pad_add_fusion.place, bf16[8,16,3072]{2,1,0:T(8,128)(2,1)S(1)} %all-to-all-done.2.parts_ref, bf16[16,3072]{1,0:T(8,128)(2,1)S(1)} %bitcast.39, f32[1,3072]{1,0:T(1,128)S(1)} %copy-done.4, f32[1,3072]{1,0:T(1,128)S(1)} %copy-done.5, f32[1,3072]{1,0:T(1,128)S(1)} %copy-done.6, ...), custom_call_target="tpu_custom_call" | custom-call | tf_op jit(solution)/shard_map/latents/pallas_call | solution.py:315
  73.4 18.3 %all_to_all.26 = bf16[64,8,128]{2,1,0:T(8,128)(2,1)} all-to-all(bf16[64,8,128]{2,1,0:T(8,128)(2,1)S(1)} %bitcast.38), channel_id=1, replica_groups=mesh['seq'=8,'chan'=16,'frame'=4] {'chan','frame'}, dimensions={0} | all-to-all | bytes 262144 | tf_op jit(solution)/shard_map/all_to_all | solution.py:332
  91.7 4.8 %all-to-all-start.4 = ((bf16[64,8,128]{2,1,0:T(8,128)(2,1)}), bf16[64,8,128]{2,1,0:T(8,128)(2,1)S(1)}, u32[]{:S(2)}, u32[]{:S(2)}) async-start(bf16[64,8,128]{2,1,0:T(8,128)(2,1)} %all_to_all.26), calls=%async_computation.4 | async-start | bytes 262144 | tf_op jit(solution)/shard_map/all_to_all | solution.py:333
  96.4 0.1 copy.43.bias_ref
  96.5 9.0 %all-to-all-done.4 = bf16[64,8,128]{2,1,0:T(8,128)(2,1)S(1)} async-done(((bf16[64,8,128]{2,1,0:T(8,128)(2,1)}), bf16[64,8,128]{2,1,0:T(8,128)(2,1)S(1)}, u32[]{:S(2)}, u32[]{:S(2)}) %all-to-all-start.4) | async-done | bytes 131104 | tf_op jit(solution)/shard_map/all_to_all | solution.py:333
  105.5 5.2 %decode.1 = bf16[2,2,32,256]{3,2,1,0:T(8,128)(2,1)} custom-call(s32[3]{0:T(128)S(1)} %pad_add_fusion.place, bf16[512,128]{1,0:T(8,128)(2,1)S(1)} %bitcast.37, bf16[16,32,512]{2,1,0:T(8,128)(2,1)S(1)} %pad_maximum_fusion.table_ref, bf16[27,32,512]{2,1,0:T(8,128)(2,1)S(1)} %bitcast.36, f32[32,1]{1,0:T(8,128)S(1)} %copy.43.bias_ref), custom_call_target="tpu_custom_call" | custom-call | tf_op jit(solution)/shard_map/decode/pallas_call | solution.py:334
  (20 shorter events, 0.1 us)
Async XLA Ops:
  0.0 17.0 %copy-start.9 = (f32[32]{0:T(128)S(1)}, f32[32]{0:T(128)}, u32[]{:S(2)}) copy-start(f32[32]{0:T(128)} %param.33) | copy-start | bytes 388
  0.0 17.3 %copy-start.10 = (f32[32]{0:T(128)S(1)}, f32[32]{0:T(128)}, u32[]{:S(2)}) copy-start(f32[32]{0:T(128)} %param.34) | copy-start | bytes 388
  0.0 17.6 %copy-start.11 = (f32[32]{0:T(128)S(1)}, f32[32]{0:T(128)}, u32[]{:S(2)}) copy-start(f32[32]{0:T(128)} %param.35) | copy-start | bytes 388
  2.1 44.2 %copy-start = (bf16[3,128,3072]{2,1,0:T(8,128)(2,1)S(1)}, bf16[3,128,3072]{2,1,0:T(8,128)(2,1)}, u32[]{:S(2)}) copy-start(bf16[3,128,3072]{2,1,0:T(8,128)(2,1)} %weight_ref.2) | copy-start | bytes 7077892
  2.1 32.5 %all-to-all-start = ((bf16[32,64,128]{2,1,0:T(8,128)(2,1)}), bf16[32,64,128]{2,1,0:T(8,128)(2,1)S(1)}, u32[]{:S(2)}, u32[]{:S(2)}) async-start(bf16[32,64,128]{2,1,0:T(8,128)(2,1)} %pack_rows.1), calls=%async_computation | async-start | bytes 1048576 | tf_op jit(solution)/shard_map/all_to_all | solution.py:292
  18.1 10.6 %collective-permute-start = (bf16[1,32,512]{2,1,0:T(8,128)(2,1)S(1)}, bf16[1,32,512]{2,1,0:T(8,128)(2,1)S(1)}, u32[]{:S(2)}, u32[]{:S(2)}) collective-permute-start(bf16[1,32,512]{2,1,0:T(8,128)(2,1)S(1)} %bitcast.43), channel_id=1, source_target_pairs={{0,32},{4,36},{8,40},{12,44},{16,48},{20,52},{24,56},{28,60},{32,0... | collective-permute-start | bytes 98312 | tf_op jit(solution)/shard_map/ppermute | solution.py:270
  46.3 21.7 %copy-start.7 = (f32[64]{0:T(128)S(1)}, f32[64]{0:T(128)}, u32[]{:S(2)}) copy-start(f32[64]{0:T(128)} %param.29) | copy-start | bytes 772
  47.8 24.2 %copy-start.2 = (bf16[64,3072]{1,0:T(8,128)(2,1)S(1)}, bf16[64,3072]{1,0:T(8,128)(2,1)}, u32[]{:S(2)}) copy-start(bf16[64,3072]{1,0:T(8,128)(2,1)} %weight_ref.3) | copy-start | bytes 1179652
  47.8 24.2 %copy-start.3 = (bf16[1,2,8,3072]{3,2,1,0:T(8,128)(2,1)S(1)}, bf16[1,2,8,3072]{3,2,1,0:T(8,128)(2,1)}, u32[]{:S(2)}) copy-start(bf16[1,2,8,3072]{3,2,1,0:T(8,128)(2,1)} %param.21) | copy-start | bytes 294916
  47.8 24.2 %copy-start.4 = (f32[1,3072]{1,0:T(1,128)S(1)}, f32[1,3072]{1,0:T(1,128)}, u32[]{:S(2)}) copy-start(f32[1,3072]{1,0:T(1,128)} %gate_ref.1) | copy-start | bytes 36868
  47.8 24.2 %copy-start.5 = (f32[1,3072]{1,0:T(1,128)S(1)}, f32[1,3072]{1,0:T(1,128)}, u32[]{:S(2)}) copy-start(f32[1,3072]{1,0:T(1,128)} %shift_ref.1) | copy-start | bytes 36868
  47.8 24.2 %copy-start.6 = (f32[1,3072]{1,0:T(1,128)S(1)}, f32[1,3072]{1,0:T(1,128)}, u32[]{:S(2)}) copy-start(f32[1,3072]{1,0:T(1,128)} %scale_ref.1) | copy-start | bytes 36868
  47.8 48.6 %copy-start.8 = (f32[32]{0:T(128)S(1)}, f32[32]{0:T(128)}, u32[]{:S(2)}) copy-start(f32[32]{0:T(128)} %param.37) | copy-start | bytes 388
  47.8 57.7 %copy-start.1 = (bf16[27,512,32]{1,2,0:T(8,128)(2,1)S(1)}, bf16[27,512,32]{1,2,0:T(8,128)(2,1)}, u32[]{:S(2)}) copy-start(bf16[27,512,32]{1,2,0:T(8,128)(2,1)} %param.36) | copy-start | bytes 2654212
  47.8 24.2 %all-to-all-start.2 = ((bf16[8,16,3072]{2,1,0:T(8,128)(2,1)}), bf16[8,16,3072]{2,1,0:T(8,128)(2,1)S(1)}, u32[]{:S(2)}, u32[]{:S(2)}) async-start(bf16[8,16,3072]{2,1,0:T(8,128)(2,1)} %project.1), calls=%async_computation.2 | async-start | bytes 1572864 | tf_op jit(solution)/shard_map/all_to_all | solution.py:312
  51.5 7.7 %collective-permute-start.1 = (bf16[2,32,512]{2,1,0:T(8,128)(2,1)S(1)}, bf16[2,32,512]{2,1,0:T(8,128)(2,1)S(1)}, u32[]{:S(2)}, u32[]{:S(2)}) collective-permute-start(bf16[2,32,512]{2,1,0:T(8,128)(2,1)S(1)} %pad_maximum_fusion.3), channel_id=1, source_target_pairs={{0,16},{4,20},{8,24},{12,28},{16,0},{20,4},{24,8},{28,12},{32,48},... | collective-permute-start | bytes 196616 | tf_op jit(solution)/shard_map/ppermute | solution.py:270
  59.2 6.9 %collective-permute-start.2 = (bf16[4,32,512]{2,1,0:T(8,128)(2,1)S(1)}, bf16[4,32,512]{2,1,0:T(8,128)(2,1)S(1)}, u32[]{:S(2)}, u32[]{:S(2)}) collective-permute-start(bf16[4,32,512]{2,1,0:T(8,128)(2,1)S(1)} %pad_maximum_fusion.2), channel_id=1, source_target_pairs={{0,8},{4,12},{8,0},{12,4},{16,24},{20,28},{24,16},{28,20},{32,40},... | collective-permute-start | bytes 393224 | tf_op jit(solution)/shard_map/ppermute | solution.py:270
  66.1 3.4 %collective-permute-start.3 = (bf16[8,32,512]{2,1,0:T(8,128)(2,1)S(1)}, bf16[8,32,512]{2,1,0:T(8,128)(2,1)S(1)}, u32[]{:S(2)}, u32[]{:S(2)}) collective-permute-start(bf16[8,32,512]{2,1,0:T(8,128)(2,1)S(1)} %pad_maximum_fusion.1), channel_id=1, source_target_pairs={{0,4},{4,0},{8,12},{12,8},{16,20},{20,16},{24,28},{28,24},{32,36},... | collective-permute-start | bytes 786440 | tf_op jit(solution)/shard_map/ppermute | solution.py:270
  91.7 13.8 %all-to-all-start.4 = ((bf16[64,8,128]{2,1,0:T(8,128)(2,1)}), bf16[64,8,128]{2,1,0:T(8,128)(2,1)S(1)}, u32[]{:S(2)}, u32[]{:S(2)}) async-start(bf16[64,8,128]{2,1,0:T(8,128)(2,1)} %all_to_all.26), calls=%async_computation.4 | async-start | bytes 262144 | tf_op jit(solution)/shard_map/all_to_all | solution.py:333

commit v4 on v3

--- a/solution.py
+++ b/solution.py
@@ -68,16 +68,22 @@
     position = jnp.where(column < 512, (column >> 3) & 7, column - 512)
     limit = jnp.where(column < 512, limits[0], limits[1])
     penalty = jnp.where(position < limit, 0.0, -jnp.inf)
+    scores = []
     for frame in range(4):
         queries = rows_ref[:, frame, 0:16, :].reshape(128, HD)
-        scores = lax.dot_general(
+        products = lax.dot_general(
             queries, keys, (((1,), (1,)), ((), ())), preferred_element_type=F32
-        ) * (1.0 / math.sqrt(HD))
-        scores = scores + penalty
-        weights = jnp.exp(scores - jnp.max(scores, axis=-1, keepdims=True))
-        weight_sum = jnp.sum(weights, axis=-1, keepdims=True)
-        attended = jnp.dot(weights.astype(BF16), values, preferred_element_type=F32)
-        out_ref[frame] = (attended / weight_sum).astype(BF16)
+        )
+        scores.append(products * (1.0 / math.sqrt(HD)) + penalty)
+    weights = []
+    sums = []
+    for frame in range(4):
+        raw = jnp.exp(scores[frame] - jnp.max(scores[frame], axis=-1, keepdims=True))
+        sums.append(jnp.sum(raw, axis=-1, keepdims=True))
+        weights.append(raw.astype(BF16))
+    for frame in range(4):
+        attended = jnp.dot(weights[frame], values, preferred_element_type=F32)
+        out_ref[frame] = (attended / sums[frame]).astype(BF16)
 
 
 def project_kernel(attended_ref, weight_ref, out_ref):
@@ -158,12 +164,15 @@
     in_weight = table[:, :448].astype(BF16)
     gain = 0.5 * (table[:, 435:436] + table[:, 436:437] + table[:, 437:438])
     bias = 0.5 * (table[:, 438:439] + table[:, 439:440] + table[:, 440:441])
+    gain = jnp.broadcast_to(gain, (DCH, 128))
+    bias = jnp.broadcast_to(bias, (DCH, 128))
     row = lax.broadcasted_iota(jnp.int32, (16, 256), 0)
     ones = jnp.where(row < 3, 1.0, 0.0)
     latent_scratch[...] = latent_ref[...].astype(F32).reshape(64, 8, 128)
     lane = lax.broadcasted_iota(jnp.int32, (1, 128), 1)
     low = lane < 64
     even = (lane & 16) == 0
+    activated = []
     for video in range(2):
         fields = []
         for step in range(3):
@@ -194,15 +203,15 @@
         for tap in range(9):
             moved = shifted(stacked, tap)
             for step in range(6):
-                taps_ref[9 * step + tap] = moved[16 * step : 16 * step + 16]
+                taps_ref[video, 9 * step + tap] = moved[16 * step : 16 * step + 16]
         active = []
         for step in range(4):
-            window = taps_ref[9 * step : 9 * step + 27].reshape(432, 256)
+            window = taps_ref[video, 9 * step : 9 * step + 27].reshape(432, 256)
             window = jnp.concatenate([window, ones], axis=0).astype(BF16)
             hidden = jnp.dot(in_weight, window, preferred_element_type=F32)
             hidden = hidden.astype(BF16).astype(F32)
             if step >= 2:
-                hidden_ref[step - 2] = hidden.reshape(16, 32, 256)
+                hidden_ref[video, step - 2] = hidden.reshape(16, 32, 256)
             halves = hidden[:, :128] + hidden[:, 128:]
             total = jnp.sum(halves.reshape(GROUPS, 16, 128), axis=1)
             mean = jnp.sum(total, axis=1, keepdims=True) * (1.0 / 4096.0)
@@ -211,10 +220,19 @@
             total = jnp.sum(halves.reshape(GROUPS, 16, 128), axis=1)
             variance = jnp.sum(total, axis=1, keepdims=True) * (1.0 / 4096.0) - mean * mean
             inverse = lax.rsqrt(variance + EPSILON)
-            mean = jnp.broadcast_to(mean[:, None, :], (GROUPS, 16, 1)).reshape(DCH, 1)
-            inverse = jnp.broadcast_to(inverse[:, None, :], (GROUPS, 16, 1)).reshape(DCH, 1)
-            normed = (hidden - mean) * (inverse * gain) + bias
+            mean = jnp.broadcast_to(mean[:, :, None], (GROUPS, 16, 128)).reshape(DCH, 128)
+            factor = jnp.broadcast_to(inverse[:, :, None], (GROUPS, 16, 128)).reshape(DCH, 128) * gain
+            normed = jnp.concatenate(
+                [
+                    (hidden[:, :128] - mean) * factor + bias,
+                    (hidden[:, 128:] - mean) * factor + bias,
+                ],
+                axis=1,
+            )
             active.append((normed + normed * jnp.tanh(normed)).astype(BF16))
+        activated.append(active)
+    for video in range(2):
+        active = activated[video]
         for step in range(2):
             branch = jnp.zeros((288, 256), F32)
             for lag in range(3):
@@ -223,7 +241,7 @@
                     active[step + lag],
                     preferred_element_type=F32,
                 )
-            total = hidden_ref[step, chan] + bias_ref[...]
+            total = hidden_ref[video, step, chan] + bias_ref[...]
             for tap in range(9):
                 total += shifted(branch[32 * tap : 32 * tap + 32], tap)
             out_ref[video, step] = total.astype(BF16)
@@ -339,8 +357,8 @@
         scratch_shapes=[
             pltpu.VMEM((64, 8, 128), F32),
             pltpu.VMEM((16, 32, DCH), F32),
-            pltpu.VMEM((54, 16, 256), F32),
-            pltpu.VMEM((2, 16, 32, 256), F32),
+            pltpu.VMEM((2, 54, 16, 256), F32),
+            pltpu.VMEM((2, 2, 16, 32, 256), F32),
         ],
         compiler_params=PARAMS,
         name="decode",

time: 111 us -> 110 us (level)
  no operation moved by 1% of the time
where the time goes in v4:
time: 110 us
  starting transfers between devices  35.7 us (32%)
  waiting for transfers between devices  30.9 us (28%)
  blocking collectives  28 us (25%)
  Pallas kernels  11.1 us (10%)
  local copies, waits for them, and re-layouts  2.23 us (2%)
  between operations  1.49 us (1%)
    all_to_all x1, blocking collectives, on_device(): lax.all_to_all(latent.reshape(64, 8, 128), ('chan', 'frame'), 0, 0, tiled...  18.3 us
    all_to_all x1, starting transfers between devices, on_device(): rows = lax.all_to_all(packed, ('seq', 'frame'), 0, 0, tiled=True)  13.9 us
    ppermute x4, waiting for transfers between devices, doubled(): other = lax.ppermute(held, 'chan', [(i, i ^ bit) for i in range(16)])  13.5 us
    ppermute x4, starting transfers between devices, doubled(): other = lax.ppermute(held, 'chan', [(i, i ^ bit) for i in range(16)])  13.4 us
    all_to_all x1, blocking collectives, on_device(): attended = lax.all_to_all(attended, 'frame', 0, 0, tiled=True)  9.72 us
    all_to_all x1, waiting for transfers between devices, on_device(): latent = lax.all_to_all(latent, 'seq', 0, 0, tiled=True)  8.98 us
    all_to_all x1, waiting for transfers between devices, on_device(): rows = lax.all_to_all(packed, ('seq', 'frame'), 0, 0, tiled=True)  5.97 us
    pallas_call x1, Pallas kernels, on_device(): pl.pallas_call(decode_kernel, out_shape=jax.ShapeDtypeStruct((2, 2, 32, 2...  4.78 us
  transfers between devices with their start and end apart: 7, of which 7 were waited for; matrix products, arithmetic and copies ran while one was open for 2% of the time, Pallas kernels for 0%

profile of v4, /device:TPU:2, one launch (start us, length us, event | category | flops | bytes accessed | tf_op | source)
XLA Modules:
  0.0 109.7 jit_solution(5378947802513356817)
XLA Ops:
  0.0 2.1 %pack_rows.1 = bf16[32,64,128]{2,1,0:T(8,128)(2,1)} custom-call(bf16[1152,128]{1,0:T(8,128)(2,1)} %bitcast.41, bf16[1536,128]{1,0:T(8,128)(2,1)} %bitcast.40, f32[1,128]{1,0:T(1,128)} %bitcast.46, f32[1,128]{1,0:T(1,128)} %bitcast.47), custom_call_target="tpu_custom_call" | custom-call | tf_op jit(solution)/shard_map/pack_rows/pallas_call | solution.py:291
  2.1 13.9 %all-to-all-start = ((bf16[32,64,128]{2,1,0:T(8,128)(2,1)}), bf16[32,64,128]{2,1,0:T(8,128)(2,1)S(1)}, u32[]{:S(2)}, u32[]{:S(2)}) async-start(bf16[32,64,128]{2,1,0:T(8,128)(2,1)} %pack_rows.1), calls=%async_computation | async-start | bytes 1048576 | tf_op jit(solution)/shard_map/all_to_all | solution.py:310
  16.0 1.0 copy.32
  17.0 0.0 copy-done.9
  17.0 0.1 copy.33
  17.1 0.1 copy.34
  17.2 0.1 copy.35
  17.3 0.0 copy-done.10
  17.4 0.1 copy.36
  17.5 0.1 copy.37
  17.6 0.1 copy.38
  17.7 0.0 copy-done.11
  17.7 0.1 copy.39
  17.8 0.1 copy.40
  17.9 0.1 copy.41
  18.0 0.1 concatenate.21
  18.1 5.0 %collective-permute-start = (bf16[1,32,512]{2,1,0:T(8,128)(2,1)S(1)}, bf16[1,32,512]{2,1,0:T(8,128)(2,1)S(1)}, u32[]{:S(2)}, u32[]{:S(2)}) collective-permute-start(bf16[1,32,512]{2,1,0:T(8,128)(2,1)S(1)} %bitcast.43), channel_id=1, source_target_pairs={{0,32},{4,36},{8,40},{12,44},{16,48},{20,52},{24,56},{28,60},{32,0... | collective-permute-start | bytes 98312 | tf_op jit(solution)/shard_map/ppermute | solution.py:288
  24.4 0.1 pad_add_fusion.1.limits
  24.5 4.2 %collective-permute-done = bf16[1,32,512]{2,1,0:T(8,128)(2,1)S(1)} collective-permute-done((bf16[1,32,512]{2,1,0:T(8,128)(2,1)S(1)}, bf16[1,32,512]{2,1,0:T(8,128)(2,1)S(1)}, u32[]{:S(2)}, u32[]{:S(2)}) %collective-permute-start) | collective-permute-done | bytes 32800 | tf_op jit(solution)/shard_map/ppermute | solution.py:288
  28.7 6.0 %all-to-all-done = bf16[32,64,128]{2,1,0:T(8,128)(2,1)S(1)} async-done(((bf16[32,64,128]{2,1,0:T(8,128)(2,1)}), bf16[32,64,128]{2,1,0:T(8,128)(2,1)S(1)}, u32[]{:S(2)}, u32[]{:S(2)}) %all-to-all-start) | async-done | bytes 524320 | tf_op jit(solution)/shard_map/all_to_all | solution.py:310
  34.6 1.3 %attend.1 = bf16[4,128,128]{2,1,0:T(8,128)(2,1)S(1)} custom-call(s32[2]{0:T(128)S(1)} %pad_add_fusion.1.limits, bf16[8,4,64,128]{3,2,1,0:T(8,128)(2,1)S(1)} %bitcast.35), custom_call_target="tpu_custom_call" | custom-call | tf_op jit(solution)/shard_map/attend/pallas_call | solution.py:313
  36.0 9.7 %all_to_all.25.attended_ref = bf16[4,128,128]{2,1,0:T(8,128)(2,1)S(1)} all-to-all(bf16[4,128,128]{2,1,0:T(8,128)(2,1)S(1)} %attend.1), channel_id=1, replica_groups=mesh['seq'=8,'chan'=16,'frame'=4] {'frame'}, dimensions={0} | all-to-all | bytes 262144 | tf_op jit(solution)/shard_map/all_to_all | solution.py:321
  45.7 0.0 copy-done
  45.7 1.5 %project.1 = bf16[8,16,3072]{2,1,0:T(8,128)(2,1)} custom-call(bf16[4,128,128]{2,1,0:T(8,128)(2,1)S(1)} %all_to_all.25.attended_ref, bf16[3,128,3072]{2,1,0:T(8,128)(2,1)S(1)} %copy-done), custom_call_target="tpu_custom_call" | custom-call | tf_op jit(solution)/shard_map/project/pallas_call | solution.py:322
  47.2 0.0 copy-start.6
  47.2 0.0 copy-start.8
  47.2 0.0 copy-start.1
  47.2 3.7 %all-to-all-start.2 = ((bf16[8,16,3072]{2,1,0:T(8,128)(2,1)}), bf16[8,16,3072]{2,1,0:T(8,128)(2,1)S(1)}, u32[]{:S(2)}, u32[]{:S(2)}) async-start(bf16[8,16,3072]{2,1,0:T(8,128)(2,1)} %project.1), calls=%async_computation.2 | async-start | bytes 1572864 | tf_op jit(solution)/shard_map/all_to_all | solution.py:330
  50.9 4.0 %collective-permute-start.1 = (bf16[2,32,512]{2,1,0:T(8,128)(2,1)S(1)}, bf16[2,32,512]{2,1,0:T(8,128)(2,1)S(1)}, u32[]{:S(2)}, u32[]{:S(2)}) collective-permute-start(bf16[2,32,512]{2,1,0:T(8,128)(2,1)S(1)} %pad_maximum_fusion.3), channel_id=1, source_target_pairs={{0,16},{4,20},{8,24},{12,28},{16,0},{20,4},{24,8},{28,12},{32,48},... | collective-permute-start | bytes 196616 | tf_op jit(solution)/shard_map/ppermute | solution.py:288
  55.0 3.6 %collective-permute-done.1 = bf16[2,32,512]{2,1,0:T(8,128)(2,1)S(1)} collective-permute-done((bf16[2,32,512]{2,1,0:T(8,128)(2,1)S(1)}, bf16[2,32,512]{2,1,0:T(8,128)(2,1)S(1)}, u32[]{:S(2)}, u32[]{:S(2)}) %collective-permute-start.1) | collective-permute-done | bytes 65568 | tf_op jit(solution)/shard_map/ppermute | solution.py:288
  58.6 2.4 %collective-permute-start.2 = (bf16[4,32,512]{2,1,0:T(8,128)(2,1)S(1)}, bf16[4,32,512]{2,1,0:T(8,128)(2,1)S(1)}, u32[]{:S(2)}, u32[]{:S(2)}) collective-permute-start(bf16[4,32,512]{2,1,0:T(8,128)(2,1)S(1)} %pad_maximum_fusion.2), channel_id=1, source_target_pairs={{0,8},{4,12},{8,0},{12,4},{16,24},{20,28},{24,16},{28,20},{32,40},... | collective-permute-start | bytes 393224 | tf_op jit(solution)/shard_map/ppermute | solution.py:288
  61.1 4.4 %collective-permute-done.2 = bf16[4,32,512]{2,1,0:T(8,128)(2,1)S(1)} collective-permute-done((bf16[4,32,512]{2,1,0:T(8,128)(2,1)S(1)}, bf16[4,32,512]{2,1,0:T(8,128)(2,1)S(1)}, u32[]{:S(2)}, u32[]{:S(2)}) %collective-permute-start.2) | collective-permute-done | bytes 131104 | tf_op jit(solution)/shard_map/ppermute | solution.py:288
  65.5 1.9 %collective-permute-start.3 = (bf16[8,32,512]{2,1,0:T(8,128)(2,1)S(1)}, bf16[8,32,512]{2,1,0:T(8,128)(2,1)S(1)}, u32[]{:S(2)}, u32[]{:S(2)}) collective-permute-start(bf16[8,32,512]{2,1,0:T(8,128)(2,1)S(1)} %pad_maximum_fusion.1), channel_id=1, source_target_pairs={{0,4},{4,0},{8,12},{12,8},{16,20},{20,16},{24,28},{28,24},{32,36},... | collective-permute-start | bytes 786440 | tf_op jit(solution)/shard_map/ppermute | solution.py:288
  67.5 0.0 copy-done.7
  67.5 0.1 copy.42.bias_ref
  67.6 0.1 pad_add_fusion.place
  67.6 1.3 %collective-permute-done.3 = bf16[8,32,512]{2,1,0:T(8,128)(2,1)S(1)} collective-permute-done((bf16[8,32,512]{2,1,0:T(8,128)(2,1)S(1)}, bf16[8,32,512]{2,1,0:T(8,128)(2,1)S(1)}, u32[]{:S(2)}, u32[]{:S(2)}) %collective-permute-start.3) | collective-permute-done | bytes 262176 | tf_op jit(solution)/shard_map/ppermute | solution.py:288
  69.0 0.1 pad_maximum_fusion.table_ref
  69.0 2.4 %all-to-all-done.2.parts_ref = bf16[8,16,3072]{2,1,0:T(8,128)(2,1)S(1)} async-done(((bf16[8,16,3072]{2,1,0:T(8,128)(2,1)}), bf16[8,16,3072]{2,1,0:T(8,128)(2,1)S(1)}, u32[]{:S(2)}, u32[]{:S(2)}) %all-to-all-start.2) | async-done | bytes 786464 | tf_op jit(solution)/shard_map/all_to_all | solution.py:330
  71.4 0.0 copy-done.2
  71.4 0.0 copy-done.3
  71.4 0.0 copy-done.4
  71.5 1.3 %latents.1 = bf16[512,128]{1,0:T(8,128)(2,1)S(1)} custom-call(s32[3]{0:T(128)S(1)} %pad_add_fusion.place, bf16[8,16,3072]{2,1,0:T(8,128)(2,1)S(1)} %all-to-all-done.2.parts_ref, bf16[16,3072]{1,0:T(8,128)(2,1)S(1)} %bitcast.39, f32[1,3072]{1,0:T(1,128)S(1)} %copy-done.4, f32[1,3072]{1,0:T(1,128)S(1)} %copy-done.5, f32[1,3072]{1,0:T(1,128)S(1)} %copy-done.6, ...), custom_call_target="tpu_custom_call" | custom-call | tf_op jit(solution)/shard_map/latents/pallas_call | solution.py:333
  72.8 18.3 %all_to_all.26 = bf16[64,8,128]{2,1,0:T(8,128)(2,1)} all-to-all(bf16[64,8,128]{2,1,0:T(8,128)(2,1)S(1)} %bitcast.38), channel_id=1, replica_groups=mesh['seq'=8,'chan'=16,'frame'=4] {'chan','frame'}, dimensions={0} | all-to-all | bytes 262144 | tf_op jit(solution)/shard_map/all_to_all | solution.py:350
  91.1 4.7 %all-to-all-start.4 = ((bf16[64,8,128]{2,1,0:T(8,128)(2,1)}), bf16[64,8,128]{2,1,0:T(8,128)(2,1)S(1)}, u32[]{:S(2)}, u32[]{:S(2)}) async-start(bf16[64,8,128]{2,1,0:T(8,128)(2,1)} %all_to_all.26), calls=%async_computation.4 | async-start | bytes 262144 | tf_op jit(solution)/shard_map/all_to_all | solution.py:351
  95.8 0.1 copy.43.bias_ref
  95.9 9.0 %all-to-all-done.4 = bf16[64,8,128]{2,1,0:T(8,128)(2,1)S(1)} async-done(((bf16[64,8,128]{2,1,0:T(8,128)(2,1)}), bf16[64,8,128]{2,1,0:T(8,128)(2,1)S(1)}, u32[]{:S(2)}, u32[]{:S(2)}) %all-to-all-start.4) | async-done | bytes 131104 | tf_op jit(solution)/shard_map/all_to_all | solution.py:351
  104.9 4.8 %decode.1 = bf16[2,2,32,256]{3,2,1,0:T(8,128)(2,1)} custom-call(s32[3]{0:T(128)S(1)} %pad_add_fusion.place, bf16[512,128]{1,0:T(8,128)(2,1)S(1)} %bitcast.37, bf16[16,32,512]{2,1,0:T(8,128)(2,1)S(1)} %pad_maximum_fusion.table_ref, bf16[27,32,512]{2,1,0:T(8,128)(2,1)S(1)} %bitcast.36, f32[32,1]{1,0:T(8,128)S(1)} %copy.43.bias_ref), custom_call_target="tpu_custom_call" | custom-call | tf_op jit(solution)/shard_map/decode/pallas_call | solution.py:352
  (20 shorter events, 0.1 us)
Async XLA Ops:
  0.0 17.0 %copy-start.9 = (f32[32]{0:T(128)S(1)}, f32[32]{0:T(128)}, u32[]{:S(2)}) copy-start(f32[32]{0:T(128)} %param.33) | copy-start | bytes 388
  0.0 17.3 %copy-start.10 = (f32[32]{0:T(128)S(1)}, f32[32]{0:T(128)}, u32[]{:S(2)}) copy-start(f32[32]{0:T(128)} %param.34) | copy-start | bytes 388
  0.0 17.6 %copy-start.11 = (f32[32]{0:T(128)S(1)}, f32[32]{0:T(128)}, u32[]{:S(2)}) copy-start(f32[32]{0:T(128)} %param.35) | copy-start | bytes 388
  2.1 43.6 %copy-start = (bf16[3,128,3072]{2,1,0:T(8,128)(2,1)S(1)}, bf16[3,128,3072]{2,1,0:T(8,128)(2,1)}, u32[]{:S(2)}) copy-start(bf16[3,128,3072]{2,1,0:T(8,128)(2,1)} %weight_ref.2) | copy-start | bytes 7077892
  2.1 32.5 %all-to-all-start = ((bf16[32,64,128]{2,1,0:T(8,128)(2,1)}), bf16[32,64,128]{2,1,0:T(8,128)(2,1)S(1)}, u32[]{:S(2)}, u32[]{:S(2)}) async-start(bf16[32,64,128]{2,1,0:T(8,128)(2,1)} %pack_rows.1), calls=%async_computation | async-start | bytes 1048576 | tf_op jit(solution)/shard_map/all_to_all | solution.py:310
  18.1 10.6 %collective-permute-start = (bf16[1,32,512]{2,1,0:T(8,128)(2,1)S(1)}, bf16[1,32,512]{2,1,0:T(8,128)(2,1)S(1)}, u32[]{:S(2)}, u32[]{:S(2)}) collective-permute-start(bf16[1,32,512]{2,1,0:T(8,128)(2,1)S(1)} %bitcast.43), channel_id=1, source_target_pairs={{0,32},{4,36},{8,40},{12,44},{16,48},{20,52},{24,56},{28,60},{32,0... | collective-permute-start | bytes 98312 | tf_op jit(solution)/shard_map/ppermute | solution.py:288
  45.7 21.7 %copy-start.7 = (f32[64]{0:T(128)S(1)}, f32[64]{0:T(128)}, u32[]{:S(2)}) copy-start(f32[64]{0:T(128)} %param.29) | copy-start | bytes 772
  47.2 24.2 %copy-start.2 = (bf16[64,3072]{1,0:T(8,128)(2,1)S(1)}, bf16[64,3072]{1,0:T(8,128)(2,1)}, u32[]{:S(2)}) copy-start(bf16[64,3072]{1,0:T(8,128)(2,1)} %weight_ref.3) | copy-start | bytes 1179652
  47.2 24.2 %copy-start.3 = (bf16[1,2,8,3072]{3,2,1,0:T(8,128)(2,1)S(1)}, bf16[1,2,8,3072]{3,2,1,0:T(8,128)(2,1)}, u32[]{:S(2)}) copy-start(bf16[1,2,8,3072]{3,2,1,0:T(8,128)(2,1)} %param.21) | copy-start | bytes 294916
  47.2 24.2 %copy-start.4 = (f32[1,3072]{1,0:T(1,128)S(1)}, f32[1,3072]{1,0:T(1,128)}, u32[]{:S(2)}) copy-start(f32[1,3072]{1,0:T(1,128)} %gate_ref.1) | copy-start | bytes 36868
  47.2 24.2 %copy-start.5 = (f32[1,3072]{1,0:T(1,128)S(1)}, f32[1,3072]{1,0:T(1,128)}, u32[]{:S(2)}) copy-start(f32[1,3072]{1,0:T(1,128)} %shift_ref.1) | copy-start | bytes 36868
  47.2 24.2 %copy-start.6 = (f32[1,3072]{1,0:T(1,128)S(1)}, f32[1,3072]{1,0:T(1,128)}, u32[]{:S(2)}) copy-start(f32[1,3072]{1,0:T(1,128)} %scale_ref.1) | copy-start | bytes 36868
  47.2 48.6 %copy-start.8 = (f32[32]{0:T(128)S(1)}, f32[32]{0:T(128)}, u32[]{:S(2)}) copy-start(f32[32]{0:T(128)} %param.37) | copy-start | bytes 388
  47.2 57.7 %copy-start.1 = (bf16[27,512,32]{1,2,0:T(8,128)(2,1)S(1)}, bf16[27,512,32]{1,2,0:T(8,128)(2,1)}, u32[]{:S(2)}) copy-start(bf16[27,512,32]{1,2,0:T(8,128)(2,1)} %param.36) | copy-start | bytes 2654212
  47.2 24.2 %all-to-all-start.2 = ((bf16[8,16,3072]{2,1,0:T(8,128)(2,1)}), bf16[8,16,3072]{2,1,0:T(8,128)(2,1)S(1)}, u32[]{:S(2)}, u32[]{:S(2)}) async-start(bf16[8,16,3072]{2,1,0:T(8,128)(2,1)} %project.1), calls=%async_computation.2 | async-start | bytes 1572864 | tf_op jit(solution)/shard_map/all_to_all | solution.py:330
  50.9 7.7 %collective-permute-start.1 = (bf16[2,32,512]{2,1,0:T(8,128)(2,1)S(1)}, bf16[2,32,512]{2,1,0:T(8,128)(2,1)S(1)}, u32[]{:S(2)}, u32[]{:S(2)}) collective-permute-start(bf16[2,32,512]{2,1,0:T(8,128)(2,1)S(1)} %pad_maximum_fusion.3), channel_id=1, source_target_pairs={{0,16},{4,20},{8,24},{12,28},{16,0},{20,4},{24,8},{28,12},{32,48},... | collective-permute-start | bytes 196616 | tf_op jit(solution)/shard_map/ppermute | solution.py:288
  58.6 6.9 %collective-permute-start.2 = (bf16[4,32,512]{2,1,0:T(8,128)(2,1)S(1)}, bf16[4,32,512]{2,1,0:T(8,128)(2,1)S(1)}, u32[]{:S(2)}, u32[]{:S(2)}) collective-permute-start(bf16[4,32,512]{2,1,0:T(8,128)(2,1)S(1)} %pad_maximum_fusion.2), channel_id=1, source_target_pairs={{0,8},{4,12},{8,0},{12,4},{16,24},{20,28},{24,16},{28,20},{32,40},... | collective-permute-start | bytes 393224 | tf_op jit(solution)/shard_map/ppermute | solution.py:288
  65.5 3.4 %collective-permute-start.3 = (bf16[8,32,512]{2,1,0:T(8,128)(2,1)S(1)}, bf16[8,32,512]{2,1,0:T(8,128)(2,1)S(1)}, u32[]{:S(2)}, u32[]{:S(2)}) collective-permute-start(bf16[8,32,512]{2,1,0:T(8,128)(2,1)S(1)} %pad_maximum_fusion.1), channel_id=1, source_target_pairs={{0,4},{4,0},{8,12},{12,8},{16,20},{20,16},{24,28},{28,24},{32,36},... | collective-permute-start | bytes 786440 | tf_op jit(solution)/shard_map/ppermute | solution.py:288
  91.1 13.8 %all-to-all-start.4 = ((bf16[64,8,128]{2,1,0:T(8,128)(2,1)}), bf16[64,8,128]{2,1,0:T(8,128)(2,1)S(1)}, u32[]{:S(2)}, u32[]{:S(2)}) async-start(bf16[64,8,128]{2,1,0:T(8,128)(2,1)} %all_to_all.26), calls=%async_computation.4 | async-start | bytes 262144 | tf_op jit(solution)/shard_map/all_to_all | solution.py:351
